TPU v7x, 256 devices: a whole 4x4x8 slice. The times are simulated.
256 devices in a mesh: gx: 32 (over x_lo, z, core), gy: 8 (over x_hi, y).
Axes of the slice: x: 4 (x_hi: 2, x_lo: 2; x = x_hi * 2 + x_lo), y: 4, z: 8, core: 2. Of those that a mesh axis runs over, the one named last changes fastest.
Arguments:
- angles: float32 [8, 4, 512, 2048], P(None, None, 'gx', 'gy'), may hold values from -3.140625 to 3.140625
- bond_flux: int32 [7, 512, 2048], P(None, 'gx', 'gy'), may hold values from 0 to 63
- coupling: float32 [512, 2048], P('gx', 'gy'), may hold values from 0.2 to 0.8
Outputs:
- evolved: float32 [2, 8, 4, 512, 2048], P(None, None, None, 'gx', 'gy')
- moments: float32 [16, 2, 8], replicated
All inputs are finite; a program needn't handle non-finite values.
Results may differ from a plain program's by a relative error of at most 0.0003.
Values sent between devices are 32-bit elements; how exact they have to be, the bound alone decides.
A program may use at most 192 MiB of HBM per device.

v0:
```python
import math

import jax
import jax.numpy as jnp
from jax import lax
from jax.sharding import PartitionSpec as P

TERMS = 16
QUANTA = 64


energy_scale = 4.0
phase_span = 12.0


def with_halo(array, sides, width):
    for axis, dim in sides:
        peers, length = (lax.axis_size(axis), array.shape[dim])
        up = [(i, (i + 1) % peers) for i in range(peers - 1)]
        down = [(j, i) for i, j in up]
        last = lax.slice_in_dim(array, length - width, length, axis=dim)
        first = lax.slice_in_dim(array, 0, width, axis=dim)
        before = lax.ppermute(last, axis, up)
        after = lax.ppermute(first, axis, down)
        array = jnp.concatenate([before, array, after], axis=dim)
    return array


def bessel_value(degree, argument):
    running = 0.0
    for number in range(60):
        running += (
            (-1.0) ** number
            * (argument / 2.0) ** (2 * number + degree)
            / (math.factorial(number) * math.factorial(number + degree))
        )
    return running


def chebyshev_weights(count):
    weights_real = []
    weights_imag = []
    for degree in range(count):
        amplitude = bessel_value(degree, phase_span) * (1.0 if degree == 0 else 2.0)
        quarter = degree % 4
        weights_real.append(amplitude if quarter == 0 else -amplitude if quarter == 2 else 0.0)
        weights_imag.append(-amplitude if quarter == 1 else amplitude if quarter == 3 else 0.0)
    return (weights_real, weights_imag)


def rotate(cosine_part, sine_part, pair, sign):
    return (
        cosine_part * pair[0] - sign * sine_part * pair[1],
        sign * sine_part * pair[0] + cosine_part * pair[1],
    )


def orbital(complex_field, position):
    return (complex_field[0][:, position], complex_field[1][:, position])


def summed(one_pair, two_pair, three_pair):
    return (one_pair[0] + two_pair[0] + three_pair[0], one_pair[1] + two_pair[1] + three_pair[1])


def negated(pair):
    return (-pair[0], -pair[1])


def times_unit(pair):
    return (-pair[1], pair[0])


def assemble(site_a1, site_b2, site_b1, site_a2):
    real_part = jnp.stack([site_a1[0], site_b2[0], site_b1[0], site_a2[0]], axis=1)
    imag_part = jnp.stack([site_a1[1], site_b2[1], site_b1[1], site_a2[1]], axis=1)
    return jnp.stack([real_part, imag_part])


def apply_ham(state_field, nearby, tables):
    lower_x, upper_x, lower_y, upper_y = nearby
    cos_own, sin_own, cos_near, sin_near, coupling = tables
    site_a1 = negated(
        summed(
            rotate(cos_own[0], sin_own[0], orbital(state_field, 2), 1.0),
            rotate(cos_own[1], sin_own[1], orbital(lower_x, 0), 1.0),
            rotate(cos_own[2], sin_own[2], orbital(lower_y, 0), 1.0),
        )
    )
    site_b2 = negated(
        summed(
            rotate(cos_own[3], sin_own[3], orbital(state_field, 3), -1.0),
            rotate(cos_near[2], sin_near[2], orbital(lower_x, 1), -1.0),
            rotate(cos_near[3], sin_near[3], orbital(lower_y, 1), -1.0),
        )
    )
    hop_b1 = negated(
        summed(
            rotate(cos_own[0], sin_own[0], orbital(state_field, 0), -1.0),
            rotate(cos_near[0], sin_near[0], orbital(upper_x, 0), -1.0),
            rotate(cos_near[1], sin_near[1], orbital(upper_y, 0), -1.0),
        )
    )
    inter_b1 = rotate(cos_own[6], sin_own[6], orbital(state_field, 3), 1.0)
    site_b1 = (hop_b1[0] + coupling * inter_b1[0], hop_b1[1] + coupling * inter_b1[1])
    hop_a2 = negated(
        summed(
            rotate(cos_own[3], sin_own[3], orbital(state_field, 1), 1.0),
            rotate(cos_own[4], sin_own[4], orbital(upper_x, 1), 1.0),
            rotate(cos_own[5], sin_own[5], orbital(upper_y, 1), 1.0),
        )
    )
    inter_a2 = rotate(cos_own[6], sin_own[6], orbital(state_field, 2), -1.0)
    site_a2 = (hop_a2[0] + coupling * inter_a2[0], hop_a2[1] + coupling * inter_a2[1])
    return assemble(site_a1, site_b2, site_b1, site_a2)


def apply_vel(nearby, tables):
    lower_x, upper_x, lower_y, upper_y = nearby
    cos_own, sin_own, cos_near, sin_near, coupling = tables
    site_a1 = times_unit(negated(rotate(cos_own[1], sin_own[1], orbital(lower_x, 0), 1.0)))
    site_b1 = times_unit(rotate(cos_near[0], sin_near[0], orbital(upper_x, 0), -1.0))
    site_a2 = times_unit(rotate(cos_own[4], sin_own[4], orbital(upper_x, 1), 1.0))
    site_b2 = times_unit(negated(rotate(cos_near[2], sin_near[2], orbital(lower_x, 1), -1.0)))
    return assemble(site_a1, site_b2, site_b1, site_a2)


def intersection(velocity, current):
    real_part = jnp.sum(velocity[0] * current[0] + velocity[1] * current[1], axis=(1, 2, 3))
    imag_part = jnp.sum(velocity[0] * current[1] - velocity[1] * current[0], axis=(1, 2, 3))
    return jnp.stack([real_part, imag_part])


def scaled(complex_field, weight_real, weight_imag):
    return jnp.stack(
        [
            weight_real * complex_field[0] - weight_imag * complex_field[1],
            weight_real * complex_field[1] + weight_imag * complex_field[0],
        ]
    )


def neighbours(state_field):
    padded = with_halo(state_field, (("gx", 3), ("gy", 4)), 1)
    return (
        padded[:, :, 2:4, :-2, 1:-1],
        padded[:, :, 0:2, 2:, 1:-1],
        padded[:, :, 2:4, 1:-1, :-2],
        padded[:, :, 0:2, 1:-1, 2:],
    )


def record(store, degree, local_value):
    local_value = lax.psum(local_value, ("gx", "gy"))
    return store.at[degree].set(local_value)


def per_device(angles, bond_flux, coupling):
    phase_step = 2.0 * math.pi / QUANTA
    theta = bond_flux.astype(jnp.float32) * phase_step
    rim_flux = with_halo(
        jnp.stack([bond_flux[1], bond_flux[2], bond_flux[4], bond_flux[5]]),
        (("gx", 1), ("gy", 2)),
        1,
    )
    near_flux = jnp.stack(
        [
            rim_flux[0, 2:, 1:-1],
            rim_flux[1, 1:-1, 2:],
            rim_flux[2, :-2, 1:-1],
            rim_flux[3, 1:-1, :-2],
        ]
    )
    theta_near = near_flux.astype(jnp.float32) * phase_step
    tables = (jnp.cos(theta), jnp.sin(theta), jnp.cos(theta_near), jnp.sin(theta_near), coupling)
    weights_real, weights_imag = chebyshev_weights(TERMS)
    weight_table_real = jnp.array(weights_real, jnp.float32)
    weight_table_imag = jnp.array(weights_imag, jnp.float32)
    cells_total = (
        4.0 * angles.shape[2] * angles.shape[3] * lax.axis_size("gx") * lax.axis_size("gy")
    )
    norm_factor = 1.0 / math.sqrt(cells_total)
    start = jnp.stack([jnp.cos(angles), jnp.sin(angles)])
    start_near = neighbours(start)
    velocity = apply_vel(start_near, tables)
    store = jnp.zeros((TERMS, 2, angles.shape[0]), jnp.float32)
    store = record(store, 0, intersection(velocity, start))
    total_sum = scaled(start, weights_real[0], weights_imag[0])
    current = apply_ham(start, start_near, tables) / energy_scale
    total_sum = total_sum + scaled(current, weights_real[1], weights_imag[1])
    store = record(store, 1, intersection(velocity, current))

    def advance(degree, carry):
        previous, present, running, kept = carry
        following = 2.0 * apply_ham(present, neighbours(present), tables) / energy_scale - previous
        running = running + scaled(following, weight_table_real[degree], weight_table_imag[degree])
        kept = record(kept, degree, intersection(velocity, following))
        return (present, following, running, kept)

    previous, current, total_sum, store = lax.fori_loop(
        2, TERMS, advance, (start, current, total_sum, store)
    )
    return (total_sum, store * norm_factor)


def solution(mesh):
    in_specs = (P(None, None, "gx", "gy"), P(None, "gx", "gy"), P("gx", "gy"))
    out_specs = (P(None, None, None, "gx", "gy"), P())
    return jax.shard_map(
        per_device, mesh=mesh, in_specs=in_specs, out_specs=out_specs, check_vma=False
    )
```

profile of v0, /device:TPU:1, one launch (start us, length us, event | category | flops | bytes accessed | tf_op | source)
XLA Modules:
  0.0 1850.4 jit_solution(12320064767714035013)
XLA Ops:
  1.4 4.9 collective-permute-start.8
  11.3 3.8 collective-permute-start.4
  30.4 3.8 collective-permute-start.6
  54.1 87.4 %all-reduce.1 = (f32[1,2,8]{2,1,0:T(2,128)S(1)}, f32[1,2,8]{2,1,0:T(2,128)S(1)}) all-reduce(f32[1,2,8]{2,1,0:T(2,128)S(1)} %maximum_bitcast_fusion.11, f32[1,2,8]{2,1,0:T(2,128)S(1)} %maximum_bitcast_fusion.12), channel_id=1, replica_groups=mesh['gx'=32,'gy'=8] {'gx','gy'}, use_global_device_ids=true, to_apply=%region_2.0 | all-reduce | flops 32 | bytes 256 | tf_op jit(solution)/shard_map/psum | solution.py:154
  143.8 1705.1 %while.27 = (s32[]{:T(128)}, f32[2,8,4,16,256]{4,1,3,2,0:T(8,128)}, f32[2,8,4,16,256]{4,3,2,1,0:T(8,128)S(1)}, f32[2,8,4,16,256]{4,3,2,1,0:T(8,128)}, f32[16,2,8...) while((s32[]{:T(128)}, f32[2,8,4,16,256]{4,1,3,2,0:T(8,128)}, ...), condition=%wide.region_11.12_spmd.clone, body=%wide.region_6.11_spmd.sunk.clone.sunk | while | flops 8024119 | bytes 68051568 | solution.py:200
  145.5 3.9 collective-permute-start.1
  181.0 80.1 %psum.36 = f32[1,2,8]{2,1,0:T(2,128)S(1)} all-reduce(f32[1,2,8]{2,1,0:T(2,128)S(1)} %maximum_bitcast_fusion.20), channel_id=1, replica_groups=mesh['gx'=32,'gy'=8] {'gx','gy'}, use_global_device_ids=true, to_apply=%region_10.0 | all-reduce | flops 16 | bytes 128 | tf_op jit(solution)/shard_map/while/body/eval_jaxpr/psum | solution.py:154
  267.6 4.0 collective-permute-start.1
  302.5 80.7 %psum.36 = f32[1,2,8]{2,1,0:T(2,128)S(1)} all-reduce(f32[1,2,8]{2,1,0:T(2,128)S(1)} %maximum_bitcast_fusion.20), channel_id=1, replica_groups=mesh['gx'=32,'gy'=8] {'gx','gy'}, use_global_device_ids=true, to_apply=%region_10.0 | all-reduce | flops 16 | bytes 128 | tf_op jit(solution)/shard_map/while/body/eval_jaxpr/psum | solution.py:154
  424.1 80.8 %psum.36 = f32[1,2,8]{2,1,0:T(2,128)S(1)} all-reduce(f32[1,2,8]{2,1,0:T(2,128)S(1)} %maximum_bitcast_fusion.20), channel_id=1, replica_groups=mesh['gx'=32,'gy'=8] {'gx','gy'}, use_global_device_ids=true, to_apply=%region_10.0 | all-reduce | flops 16 | bytes 128 | tf_op jit(solution)/shard_map/while/body/eval_jaxpr/psum | solution.py:154
  511.4 3.6 collective-permute-start.1
  545.9 80.8 %psum.36 = f32[1,2,8]{2,1,0:T(2,128)S(1)} all-reduce(f32[1,2,8]{2,1,0:T(2,128)S(1)} %maximum_bitcast_fusion.20), channel_id=1, replica_groups=mesh['gx'=32,'gy'=8] {'gx','gy'}, use_global_device_ids=true, to_apply=%region_10.0 | all-reduce | flops 16 | bytes 128 | tf_op jit(solution)/shard_map/while/body/eval_jaxpr/psum | solution.py:154
  633.2 3.6 collective-permute-start.1
  667.7 80.8 %psum.36 = f32[1,2,8]{2,1,0:T(2,128)S(1)} all-reduce(f32[1,2,8]{2,1,0:T(2,128)S(1)} %maximum_bitcast_fusion.20), channel_id=1, replica_groups=mesh['gx'=32,'gy'=8] {'gx','gy'}, use_global_device_ids=true, to_apply=%region_10.0 | all-reduce | flops 16 | bytes 128 | tf_op jit(solution)/shard_map/while/body/eval_jaxpr/psum | solution.py:154
  789.4 80.8 %psum.36 = f32[1,2,8]{2,1,0:T(2,128)S(1)} all-reduce(f32[1,2,8]{2,1,0:T(2,128)S(1)} %maximum_bitcast_fusion.20), channel_id=1, replica_groups=mesh['gx'=32,'gy'=8] {'gx','gy'}, use_global_device_ids=true, to_apply=%region_10.0 | all-reduce | flops 16 | bytes 128 | tf_op jit(solution)/shard_map/while/body/eval_jaxpr/psum | solution.py:154
  911.2 80.8 %psum.36 = f32[1,2,8]{2,1,0:T(2,128)S(1)} all-reduce(f32[1,2,8]{2,1,0:T(2,128)S(1)} %maximum_bitcast_fusion.20), channel_id=1, replica_groups=mesh['gx'=32,'gy'=8] {'gx','gy'}, use_global_device_ids=true, to_apply=%region_10.0 | all-reduce | flops 16 | bytes 128 | tf_op jit(solution)/shard_map/while/body/eval_jaxpr/psum | solution.py:154
  998.5 3.6 collective-permute-start.1
  1033.0 80.8 %psum.36 = f32[1,2,8]{2,1,0:T(2,128)S(1)} all-reduce(f32[1,2,8]{2,1,0:T(2,128)S(1)} %maximum_bitcast_fusion.20), channel_id=1, replica_groups=mesh['gx'=32,'gy'=8] {'gx','gy'}, use_global_device_ids=true, to_apply=%region_10.0 | all-reduce | flops 16 | bytes 128 | tf_op jit(solution)/shard_map/while/body/eval_jaxpr/psum | solution.py:154
  1154.7 80.8 %psum.36 = f32[1,2,8]{2,1,0:T(2,128)S(1)} all-reduce(f32[1,2,8]{2,1,0:T(2,128)S(1)} %maximum_bitcast_fusion.20), channel_id=1, replica_groups=mesh['gx'=32,'gy'=8] {'gx','gy'}, use_global_device_ids=true, to_apply=%region_10.0 | all-reduce | flops 16 | bytes 128 | tf_op jit(solution)/shard_map/while/body/eval_jaxpr/psum | solution.py:154
  1276.5 80.8 %psum.36 = f32[1,2,8]{2,1,0:T(2,128)S(1)} all-reduce(f32[1,2,8]{2,1,0:T(2,128)S(1)} %maximum_bitcast_fusion.20), channel_id=1, replica_groups=mesh['gx'=32,'gy'=8] {'gx','gy'}, use_global_device_ids=true, to_apply=%region_10.0 | all-reduce | flops 16 | bytes 128 | tf_op jit(solution)/shard_map/while/body/eval_jaxpr/psum | solution.py:154
  1398.2 80.8 %psum.36 = f32[1,2,8]{2,1,0:T(2,128)S(1)} all-reduce(f32[1,2,8]{2,1,0:T(2,128)S(1)} %maximum_bitcast_fusion.20), channel_id=1, replica_groups=mesh['gx'=32,'gy'=8] {'gx','gy'}, use_global_device_ids=true, to_apply=%region_10.0 | all-reduce | flops 16 | bytes 128 | tf_op jit(solution)/shard_map/while/body/eval_jaxpr/psum | solution.py:154
  1519.9 80.8 %psum.36 = f32[1,2,8]{2,1,0:T(2,128)S(1)} all-reduce(f32[1,2,8]{2,1,0:T(2,128)S(1)} %maximum_bitcast_fusion.20), channel_id=1, replica_groups=mesh['gx'=32,'gy'=8] {'gx','gy'}, use_global_device_ids=true, to_apply=%region_10.0 | all-reduce | flops 16 | bytes 128 | tf_op jit(solution)/shard_map/while/body/eval_jaxpr/psum | solution.py:154
  1641.7 80.8 %psum.36 = f32[1,2,8]{2,1,0:T(2,128)S(1)} all-reduce(f32[1,2,8]{2,1,0:T(2,128)S(1)} %maximum_bitcast_fusion.20), channel_id=1, replica_groups=mesh['gx'=32,'gy'=8] {'gx','gy'}, use_global_device_ids=true, to_apply=%region_10.0 | all-reduce | flops 16 | bytes 128 | tf_op jit(solution)/shard_map/while/body/eval_jaxpr/psum | solution.py:154
  1763.4 80.8 %psum.36 = f32[1,2,8]{2,1,0:T(2,128)S(1)} all-reduce(f32[1,2,8]{2,1,0:T(2,128)S(1)} %maximum_bitcast_fusion.20), channel_id=1, replica_groups=mesh['gx'=32,'gy'=8] {'gx','gy'}, use_global_device_ids=true, to_apply=%region_10.0 | all-reduce | flops 16 | bytes 128 | tf_op jit(solution)/shard_map/while/body/eval_jaxpr/psum | solution.py:154
  (2086 shorter events, 590.7 us)
Async XLA Ops:
  1.4 17.7 collective-permute-start.8
  6.4 12.9 collective-permute-start.7
  11.3 16.4 collective-permute-start.4
  15.1 12.6 collective-permute-start.5
  145.5 9.4 collective-permute-start.1
  159.2 9.7 collective-permute-start.2
  267.6 9.6 collective-permute-start.1
  389.6 9.2 collective-permute-start.1
  511.4 9.2 collective-permute-start.1
  524.8 9.0 collective-permute-start.2
  633.2 9.2 collective-permute-start.1
  646.6 9.0 collective-permute-start.2
  754.9 9.2 collective-permute-start.1
  876.7 9.2 collective-permute-start.1
  890.1 9.0 collective-permute-start.2
  998.5 9.2 collective-permute-start.1
  1011.9 9.0 collective-permute-start.2
  1120.1 9.2 collective-permute-start.1
  1133.6 9.0 collective-permute-start.2
  1241.9 9.2 collective-permute-start.1
  1363.6 9.2 collective-permute-start.1
  1485.3 9.2 collective-permute-start.1
  1607.1 9.2 collective-permute-start.1
  1728.9 9.2 collective-permute-start.1
  (697 other events, 2705.6 us)
where the time goes:
time: 1860 us; the launch traced here: 1850 us
  blocking collectives  1220 us (66%)
  local copies, waits for them, and re-layouts  335 us (18%)
  starting transfers between devices  146 us (8%)
  other arithmetic  136 us (7%)
    psum x15, blocking collectives, record(): local_value = lax.psum(local_value, ('gx', 'gy'))  1220 us
    while x1330, local copies, waits for them, and re-layouts  154 us
    ppermute x32, starting transfers between devices, with_halo(): before = lax.ppermute(last, axis, up)  94.4 us
    squeeze x42, local copies, waits for them, and re-layouts, orbital(): return (complex_field[0][:, position], complex_field[1][:, position])  52.8 us
    ppermute x32, starting transfers between devices, with_halo(): after = lax.ppermute(first, axis, down)  51.2 us
  transfers between devices with their start and end apart: 64, of which 2 were waited for; matrix products, arithmetic and copies ran while one was open for 9% of the time, Pallas kernels for 0%

commit v1 on v0

v1 whole, which is shorter than its diff:
```python
import functools
import math

import jax
import jax.numpy as jnp
from jax import lax
from jax.experimental import pallas as pl
from jax.experimental.pallas import tpu as pltpu
from jax.sharding import PartitionSpec as P

TERMS = 16
QUANTA = 64
PHASE_SPAN = 12.0

STATES = 8
ROWS = 16
COLS = 256
LANES = 128
HALO = 8
EXT = ROWS + 2 * HALO
PAD = EXT + 8
TILES = 3
A1, B2, B1, A2 = 0, 1, 2, 3
MESH = pl.DeviceIdType.MESH

T1C, T1S, T2C, T2S, T2BC, T2BS, T4C, T4S, T5C, T5S, T5BC, T5BS, CPL = range(13)


def bessel_value(degree, argument):
    running = 0.0
    for number in range(60):
        running += (
            (-1.0) ** number
            * (argument / 2.0) ** (2 * number + degree)
            / (math.factorial(number) * math.factorial(number + degree))
        )
    return running


EVEN = [(1.0 if m == 0 else 2.0) * (-1.0) ** m * bessel_value(2 * m, PHASE_SPAN) for m in range(TERMS // 2)]
ODD = [-2.0 * (-1.0) ** m * bessel_value(2 * m + 1, PHASE_SPAN) for m in range(TERMS // 2)]

SIN_COEF = [(-1.0) ** n * math.pi ** (2 * n + 1) / math.factorial(2 * n + 1) for n in range(6)]
COS_COEF = [(-1.0) ** n * math.pi ** (2 * n) / math.factorial(2 * n) for n in range(7)]


def turn(f):
    r = f - jnp.floor(f + 0.5)
    q = r * r
    s = SIN_COEF[-1]
    for value in reversed(SIN_COEF[:-1]):
        s = s * q + value
    s = s * r
    c = COS_COEF[-1]
    for value in reversed(COS_COEF[:-1]):
        c = c * q + value
    return 1.0 - 2.0 * s * s, 2.0 * s * c


def pick(table, m):
    value = jnp.float32(table[0])
    for at in range(1, len(table)):
        value = jnp.where(m == at, jnp.float32(table[at]), value)
    return value


def rot(c, s, v):
    return c * v[0] - s * v[1], s * v[0] + c * v[1]


def rot_back(c, s, v):
    return c * v[0] + s * v[1], c * v[1] - s * v[0]


def add(*pairs):
    re, im = pairs[0]
    for pair in pairs[1:]:
        re, im = re + pair[0], im + pair[1]
    return re, im


def kernel(
    nx, ny, gx_size, gy_size,
    ang_h, flux_h, coup_h, evo_h, mom_ref,
    ang, fli, flf, u, tab, phi, gauge, mask, vel, tot, outv, mom, pack, got, msg_x, msg_y, in_x, in_y,
    load_sem, out_sem, xs_sem, xr_sem, ps_sem, pr_sem, rxs_sem, rxr_sem, rys_sem, ryr_sem,
):
    gx, gy = lax.axis_index("gx"), lax.axis_index("gy")

    def near(dx, dy):
        return (lax.rem(gx + dx + gx_size, gx_size), lax.rem(gy + dy + gy_size, gy_size))

    lane = lax.broadcasted_iota(jnp.int32, (STATES, LANES), 1)
    first_lane, last_lane = lane == 0, lane == LANES - 1

    loads = []
    for t in range(2):
        span = pl.ds(t * LANES, LANES)
        own = pl.ds(HALO, ROWS)
        loads.append(pltpu.make_async_copy(flux_h.at[:, :, span], fli.at[t, :, own, :], load_sem.at[t, 0]))
        loads.append(pltpu.make_async_copy(coup_h.at[:, span], flf.at[t, pl.ds(7 * PAD + HALO, ROWS), :], load_sem.at[t, 1]))
        loads.append(pltpu.make_async_copy(ang_h.at[:, :, :, span], ang.at[t, :, :, own, :], load_sem.at[t, 2]))
    for copy in loads:
        copy.start()

    barrier = pltpu.get_barrier_semaphore()

    def greet_x(d, carry):
        pl.semaphore_signal(barrier, inc=1, device_id=(lax.rem(gx + d, gx_size), gy), device_id_type=MESH)
        return carry

    def greet_y(d, carry):
        pl.semaphore_signal(barrier, inc=1, device_id=(gx, lax.rem(gy + d, gy_size)), device_id_type=MESH)
        return carry

    lax.fori_loop(1, gx_size, greet_x, 0)
    lax.fori_loop(1, gy_size, greet_y, 0)
    for dx in (-1, 1):
        for dy in (-1, 1):
            pl.semaphore_signal(barrier, inc=1, device_id=near(dx, dy), device_id_type=MESH)

    zero = jnp.zeros((STATES, LANES), jnp.float32)
    for t in range(TILES):
        for plane in range(8):
            flf[t, pl.ds(plane * PAD + EXT, 8), :] = zero
        for comp in range(8):
            u[1, comp, t, 0] = zero
            u[1, comp, t, EXT - 1] = zero

    pl.semaphore_wait(barrier, gx_size - 1 + gy_size - 1 + 4)

    row_copies = []
    for side, dx in ((0, 1), (1, -1)):
        src_rows = pl.ds(ROWS - HALO, HALO) if side == 0 else pl.ds(0, HALO)
        low = 0 if side == 0 else HALO + ROWS
        for t in range(2):
            span = pl.ds(t * LANES, LANES)
            for what, (src, dst) in enumerate(
                (
                    (flux_h.at[:, src_rows, span], fli.at[t, :, pl.ds(low, HALO), :]),
                    (coup_h.at[src_rows, span], flf.at[t, pl.ds(7 * PAD + low, HALO), :]),
                    (ang_h.at[:, :, src_rows, span], ang.at[t, :, :, pl.ds(low, HALO), :]),
                )
            ):
                row_copies.append(
                    (
                        what,
                        pltpu.make_async_remote_copy(
                            src_ref=src,
                            dst_ref=dst,
                            send_sem=xs_sem.at[side, t, what],
                            recv_sem=xr_sem.at[side, t, what],
                            device_id=near(dx, 0),
                            device_id_type=MESH,
                        ),
                    )
                )
    for wanted in range(3):
        for what, copy in row_copies:
            if what == wanted:
                copy.start()

    for copy in loads:
        copy.wait()

    def flux_to_float(t, start, count):
        for plane in range(7):
            flf[t, pl.ds(plane * PAD + start, count), :] = fli[t, plane, pl.ds(start, count), :].astype(jnp.float32)

    for t in range(2):
        flux_to_float(t, HALO, ROWS)

    ang_rows = [ang.at[t].reshape(STATES * 4 * EXT, LANES) for t in range(2)]

    def ang_row(t, orb, row):
        return ang_rows[t][pl.ds(orb * EXT + row, STATES, stride=4 * EXT), :]

    group = lane // HALO
    for side in range(2):
        t = 1 - side
        for what in range(5):
            packed = zero
            for row in range(ROWS):
                if what < 4:
                    value = ang_row(t, what, HALO + row)
                else:
                    value = flf[t, pl.ds(HALO + row, 8, stride=PAD), :]
                move = (row * HALO - (LANES - HALO if side == 0 else 0)) % LANES
                if move:
                    value = pltpu.roll(value, move, 1)
                packed = jnp.where(group == row, value, packed)
            pack[side, what] = packed
    pack_copies = []
    for side, dy in ((0, 1), (1, -1)):
        for dx in (0, -1, 1):
            pack_copies.append(
                pltpu.make_async_remote_copy(
                    src_ref=pack.at[side],
                    dst_ref=got.at[side, 1 - dx],
                    send_sem=ps_sem.at[side, 1 - dx],
                    recv_sem=pr_sem.at[side, 1 - dx],
                    device_id=near(dx, dy),
                    device_id_type=MESH,
                )
            )
    for copy in pack_copies:
        copy.start()

    def flux_of(t, plane, start, count=8):
        return flf[t, pl.ds(plane * PAD + start, count), :]

    def gauge_phases(t, start):
        th0, th3, th6 = (flux_of(t, plane, start) for plane in (0, 3, 6))
        phi[0, t, pl.ds(start, 8), :] = 0.5 - th0 * (1.0 / QUANTA)
        phi[1, t, pl.ds(start, 8), :] = 0.5 + (th6 + th3) * (1.0 / QUANTA)
        phi[2, t, pl.ds(start, 8), :] = th6 * (1.0 / QUANTA)

    phi_of = {A1: 0, B2: 1, A2: 2}

    def start_value(angle, orb, t, row):
        f = angle * (0.5 / math.pi)
        if orb != B1:
            f = f + phi[phi_of[orb], t, pl.ds(row, 1), :]
        return turn(f)

    for t in range(2):
        for start in (HALO, HALO + 8):
            gauge_phases(t, start)
            for which in range(3):
                c, s = turn(phi[which, t, pl.ds(start, 8), :])
                gauge[which, 0, t, pl.ds(start - HALO, 8), :] = c
                gauge[which, 1, t, pl.ds(start - HALO, 8), :] = s

    def own_start(row, carry):
        for t in range(2):
            for orb in range(4):
                c, s = start_value(ang_row(t, orb, row), orb, t, row)
                u[0, 2 * orb, t, row] = c
                u[0, 2 * orb + 1, t, row] = s
        return carry

    lax.fori_loop(HALO, HALO + ROWS, own_start, 0)

    for what, copy in row_copies:
        if what < 2:
            copy.wait()
    for t in range(2):
        for start in (0, HALO + ROWS):
            flux_to_float(t, start, HALO)
            gauge_phases(t, start)
    for copy in pack_copies:
        copy.wait()

    def unpack(what, row):
        if row < HALO:
            part, place = 0, row + ROWS - HALO
        elif row < HALO + ROWS:
            part, place = 1, row - HALO
        else:
            part, place = 2, row - HALO - ROWS
        before, after = got[0, part, what], got[1, part, what]
        shift = (LANES - HALO - place * HALO) % LANES
        before = pltpu.roll(before, shift, 1) if shift else before
        shift = (-place * HALO) % LANES
        after = pltpu.roll(after, shift, 1) if shift else after
        return jnp.where(lane < HALO, after, jnp.where(lane >= LANES - HALO, before, 0.0))

    for row in range(EXT):
        flf[2, pl.ds(row, 8, stride=PAD), :] = unpack(4, row)
    for start in range(0, EXT, 8):
        gauge_phases(2, start)

    sub = lax.broadcasted_iota(jnp.int32, (8, LANES), 0)

    def inside(t, start, di, dj):
        i = gx * ROWS - HALO + start + sub + di
        if t < 2:
            j = gy * COLS + t * LANES + lane + dj
            good = (j >= 0) & (j < ny)
        else:
            place = lane + dj
            j = gy * COLS + jnp.where(place < LANES // 2, COLS + place, place - LANES)
            good = (j >= 0) & (j < ny) & ((place < HALO) | (place >= LANES - HALO))
        return good & (i >= 0) & (i < nx)

    def right(values):
        rolled = [pltpu.roll(value, 1, 1) for value in values]
        return [jnp.where(first_lane, rolled[(t + TILES - 1) % TILES], rolled[t]) for t in range(TILES)]

    def left(values):
        rolled = [pltpu.roll(value, LANES - 1, 1) for value in values]
        return [jnp.where(last_lane, rolled[(t + 1) % TILES], rolled[t]) for t in range(TILES)]

    for start in range(0, EXT, 8):
        rows = pl.ds(start, 8)
        th = [[flux_of(t, plane, start) for plane in range(8)] for t in range(TILES)]
        far = left([th[t][6] + th[t][3] for t in range(TILES)])
        t2, t5 = [], []
        for t in range(TILES):
            here = inside(t, start, 0, 0)
            mask[t, rows, :] = here.astype(jnp.float32)

            def bond(phase, good):
                c, s = turn(phase * (1.0 / QUANTA))
                return jnp.where(good, 0.5 * c, 0.0), jnp.where(good, 0.5 * s, 0.0)

            c, s = bond(th[t][1] - th[t][0], here & inside(t, start, -1, 0))
            tab[T1C, t, rows, :], tab[T1S, t, rows, :] = c, s
            below = flux_of(t, 6, start + 1) + flux_of(t, 3, start + 1)
            c, s = bond(th[t][4] + th[t][6] - below, here & inside(t, start, 1, 0))
            tab[T4C, t, rows, :], tab[T4S, t, rows, :] = c, s
            t2.append(bond(th[t][2] - th[t][0], here & inside(t, start, 0, -1)))
            t5.append(bond(th[t][5] + th[t][6] - far[t], here & inside(t, start, 0, 1)))
            tab[CPL, t, rows, :] = jnp.where(here, 0.5 * th[t][7], 0.0)
        for part in range(2):
            t2_back = left([t2[t][part] for t in range(TILES)])
            t5_back = right([t5[t][part] for t in range(TILES)])
            for t in range(TILES):
                tab[T2C + part, t, rows, :] = t2[t][part]
                tab[T2BC + part, t, rows, :] = t2_back[t]
                tab[T5C + part, t, rows, :] = t5[t][part]
                tab[T5BC + part, t, rows, :] = t5_back[t]

    for row in range(EXT):
        for orb in range(4):
            c, s = start_value(unpack(orb, row), orb, 2, row)
            m = mask[2, pl.ds(row, 1), :]
            u[0, 2 * orb, 2, row] = c * m
            u[0, 2 * orb + 1, 2, row] = s * m
    for what, copy in row_copies:
        if what == 2:
            copy.wait()

    def rim_start(place, carry):
        for base in (0, HALO + ROWS):
            row = base + place
            for t in range(2):
                m = mask[t, pl.ds(row, 1), :]
                for orb in range(4):
                    c, s = start_value(ang_row(t, orb, row), orb, t, row)
                    u[0, 2 * orb, t, row] = c * m
                    u[0, 2 * orb + 1, t, row] = s * m
        return carry

    lax.fori_loop(0, HALO, rim_start, 0)

    def site(buf, orb, t, row):
        return u[buf, 2 * orb, t, row], u[buf, 2 * orb + 1, t, row]

    def plane(which, t, row):
        return tab[which, t, pl.ds(row, 1), :]

    def velocity(row, carry):
        for t in range(2):
            v = rot(plane(T1C, t, row), plane(T1S, t, row), site(0, B1, t, row - 1))
            vel[2 * A1, t, row - HALO], vel[2 * A1 + 1, t, row - HALO] = v
            v = rot_back(plane(T1C, t, row + 1), plane(T1S, t, row + 1), site(0, A1, t, row + 1))
            vel[2 * B1, t, row - HALO], vel[2 * B1 + 1, t, row - HALO] = -v[0], -v[1]
            v = rot(plane(T4C, t, row), plane(T4S, t, row), site(0, B2, t, row + 1))
            vel[2 * A2, t, row - HALO], vel[2 * A2 + 1, t, row - HALO] = -v[0], -v[1]
            v = rot_back(plane(T4C, t, row - 1), plane(T4S, t, row - 1), site(0, A2, t, row - 1))
            vel[2 * B2, t, row - HALO], vel[2 * B2 + 1, t, row - HALO] = v
        return carry

    lax.fori_loop(HALO, HALO + ROWS, velocity, 0)

    def step_row(src, dst, row, first):
        here = [[site(src, orb, t, row) for orb in range(4)] for t in range(TILES)]

        def shifted(move, orb):
            re = move([here[t][orb][0] for t in range(TILES)])
            im = move([here[t][orb][1] for t in range(TILES)])
            return list(zip(re, im))

        b1_left, a2_left = shifted(right, B1), shifted(right, A2)
        a1_right, b2_right = shifted(left, A1), shifted(left, B2)
        for t in range(TILES):
            a1, b2, b1, a2 = here[t]
            cpl = plane(CPL, t, row)
            new = [None] * 4
            new[A1] = add(
                (0.5 * b1[0], 0.5 * b1[1]),
                rot(plane(T1C, t, row), plane(T1S, t, row), site(src, B1, t, row - 1)),
                rot(plane(T2C, t, row), plane(T2S, t, row), b1_left[t]),
            )
            new[B1] = add(
                (0.5 * a1[0], 0.5 * a1[1]),
                rot_back(plane(T1C, t, row + 1), plane(T1S, t, row + 1), site(src, A1, t, row + 1)),
                rot_back(plane(T2BC, t, row), plane(T2BS, t, row), a1_right[t]),
                (cpl * a2[0], cpl * a2[1]),
            )
            new[A2] = add(
                (0.5 * b2[0], 0.5 * b2[1]),
                rot(plane(T4C, t, row), plane(T4S, t, row), site(src, B2, t, row + 1)),
                rot(plane(T5C, t, row), plane(T5S, t, row), b2_right[t]),
                (cpl * b1[0], cpl * b1[1]),
            )
            new[B2] = add(
                (0.5 * a2[0], 0.5 * a2[1]),
                rot_back(plane(T4C, t, row - 1), plane(T4S, t, row - 1), site(src, A2, t, row - 1)),
                rot_back(plane(T5BC, t, row), plane(T5BS, t, row), a2_left[t]),
            )
            for orb in range(4):
                for part in range(2):
                    if first:
                        u[dst, 2 * orb + part, t, row] = 0.5 * new[orb][part]
                    else:
                        u[dst, 2 * orb + part, t, row] = new[orb][part] - u[dst, 2 * orb + part, t, row]

    def step(src, dst, low, pairs, first=False):
        def two_rows(at, carry):
            step_row(src, dst, low + 2 * at, first)
            step_row(src, dst, low + 2 * at + 1, first)
            return carry

        lax.fori_loop(0, pairs, two_rows, 0)

    def gather(m, first=False):
        if first:
            even, odd = jnp.float32(EVEN[0]), jnp.float32(ODD[0])
        else:
            even, odd = pick(EVEN, m), pick(ODD, m)

        def one_row(row, sums):
            sums = list(sums)
            for t in range(2):
                for orb in range(4):
                    now = (site(0, orb, t, HALO + row), site(1, orb, t, HALO + row))
                    vr, vi = vel[2 * orb, t, row], vel[2 * orb + 1, t, row]
                    for which, (ur, ui) in enumerate(now):
                        sums[2 * which] += vr * ur + vi * ui
                        sums[2 * which + 1] += vr * ui - vi * ur
                    re = even * now[0][0] - odd * now[1][1]
                    im = even * now[0][1] + odd * now[1][0]
                    if not first:
                        re, im = re + tot[2 * orb, t, row], im + tot[2 * orb + 1, t, row]
                    tot[2 * orb, t, row], tot[2 * orb + 1, t, row] = re, im
            return tuple(sums)

        sums = lax.fori_loop(0, ROWS, one_row, (zero,) * 4)
        for which in range(4):
            mom[4 * m + which] = sums[which]

    step(0, 1, 1, (EXT - 2) // 2, first=True)
    gather(0, first=True)

    def two_steps(m, carry):
        step(1, 0, m, EXT // 2 - m)
        step(0, 1, m + 1, EXT // 2 - 1 - m)
        gather(m)
        return carry

    lax.fori_loop(1, TERMS // 2, two_steps, 0)

    scale = 2.0 / math.sqrt(4.0 * nx * ny)
    local = zero
    for k in range(TERMS):
        re = jnp.sum(mom[2 * k + 1], axis=1, keepdims=True)
        im = -jnp.sum(mom[2 * k], axis=1, keepdims=True)
        local = jnp.where(lane == 2 * k, re, local)
        local = jnp.where(lane == 2 * k + 1, im, local)
    local = local * scale

    def spread(value, msg, slots, me, size, target, send_sem, recv_sem):
        msg[...] = value
        slots[me] = value

        def copy_to(other, slot, d):
            return pltpu.make_async_remote_copy(
                src_ref=msg,
                dst_ref=slots.at[slot],
                send_sem=send_sem.at[d],
                recv_sem=recv_sem.at[slot],
                device_id=target(other),
                device_id_type=MESH,
            )

        def send(d, carry):
            copy_to(lax.rem(me + d, size), me, d).start()
            return carry

        def finish(d, carry):
            other = lax.rem(me + d, size)
            copy_to(other, me, d).wait_send()
            copy_to(other, other, d).wait_recv()
            return carry

        lax.fori_loop(1, size, send, 0)
        return lambda: lax.fori_loop(1, size, finish, 0)

    def total(slots, size):
        value = slots[0]
        for at in range(1, size):
            value = value + slots[at]
        return value

    finish_x = spread(local, msg_x, in_x, gx, gx_size, lambda other: (other, gy), rxs_sem, rxr_sem)

    out_rows = [outv.at[t].reshape(2 * STATES * 4 * ROWS, LANES) for t in range(2)]
    outs = []
    for t in range(2):

        def finish_row(row, carry):
            for orb in range(4):
                v = tot[2 * orb, t, row], tot[2 * orb + 1, t, row]
                if orb != B1:
                    which = phi_of[orb]
                    v = rot_back(gauge[which, 0, t, pl.ds(row, 1), :], gauge[which, 1, t, pl.ds(row, 1), :], v)
                for part in range(2):
                    out_rows[t][pl.ds(part * STATES * 4 * ROWS + orb * ROWS + row, STATES, stride=4 * ROWS), :] = v[part]
            return carry

        lax.fori_loop(0, ROWS, finish_row, 0)
        copy = pltpu.make_async_copy(outv.at[t], evo_h.at[:, :, :, :, pl.ds(t * LANES, LANES)], out_sem.at[t])
        copy.start()
        outs.append(copy)

    finish_x()
    finish_y = spread(total(in_x, gx_size), msg_y, in_y, gy, gy_size, lambda other: (gx, other), rys_sem, ryr_sem)
    finish_y()
    mom_ref[...] = total(in_y, gy_size)
    for copy in outs:
        copy.wait()


def per_device(nx, ny, gx_size, gy_size, angles, bond_flux, coupling):
    f32 = jnp.float32
    tile = (STATES, LANES)
    evolved, moments = pl.pallas_call(
        functools.partial(kernel, nx, ny, gx_size, gy_size),
        out_shape=(
            jax.ShapeDtypeStruct((2, STATES, 4, ROWS, COLS), f32),
            jax.ShapeDtypeStruct(tile, f32),
        ),
        in_specs=[pl.BlockSpec(memory_space=pl.ANY)] * 3,
        out_specs=(pl.BlockSpec(memory_space=pl.ANY), pl.BlockSpec(memory_space=pltpu.VMEM)),
        scratch_shapes=[
            pltpu.VMEM((2, STATES, 4, EXT, LANES), f32),
            pltpu.VMEM((2, 7, EXT, LANES), jnp.int32),
            pltpu.VMEM((TILES, 8 * PAD, LANES), f32),
            pltpu.VMEM((2, 8, TILES, EXT) + tile, f32),
            pltpu.VMEM((13, TILES, EXT, LANES), f32),
            pltpu.VMEM((3, TILES, EXT, LANES), f32),
            pltpu.VMEM((3, 2, 2, ROWS, LANES), f32),
            pltpu.VMEM((TILES, EXT, LANES), f32),
            pltpu.VMEM((8, 2, ROWS) + tile, f32),
            pltpu.VMEM((8, 2, ROWS) + tile, f32),
            pltpu.VMEM((2, 2, STATES, 4, ROWS, LANES), f32),
            pltpu.VMEM((2 * TERMS,) + tile, f32),
            pltpu.VMEM((2, 5) + tile, f32),
            pltpu.VMEM((2, 3, 5) + tile, f32),
            pltpu.VMEM(tile, f32),
            pltpu.VMEM(tile, f32),
            pltpu.VMEM((gx_size,) + tile, f32),
            pltpu.VMEM((gy_size,) + tile, f32),
            pltpu.SemaphoreType.DMA((2, 3)),
            pltpu.SemaphoreType.DMA((2,)),
            pltpu.SemaphoreType.DMA((2, 2, 3)),
            pltpu.SemaphoreType.DMA((2, 2, 3)),
            pltpu.SemaphoreType.DMA((2, 3)),
            pltpu.SemaphoreType.DMA((2, 3)),
            pltpu.SemaphoreType.DMA((gx_size,)),
            pltpu.SemaphoreType.DMA((gx_size,)),
            pltpu.SemaphoreType.DMA((gy_size,)),
            pltpu.SemaphoreType.DMA((gy_size,)),
        ],
        compiler_params=pltpu.CompilerParams(
            collective_id=0, has_side_effects=True, vmem_limit_bytes=48 * 2**20
        ),
        name="evolve",
    )(angles, bond_flux, coupling)
    return evolved, moments[:, : 2 * TERMS].T.reshape(TERMS, 2, STATES)


def solution(mesh):
    in_specs = (P(None, None, "gx", "gy"), P(None, "gx", "gy"), P("gx", "gy"))
    out_specs = (P(None, None, None, "gx", "gy"), P())
    gx_size, gy_size = mesh.shape["gx"], mesh.shape["gy"]
    return jax.shard_map(
        functools.partial(per_device, gx_size * ROWS, gy_size * COLS, gx_size, gy_size),
        mesh=mesh,
        in_specs=in_specs,
        out_specs=out_specs,
        check_vma=False,
    )
```

time: 1860 us -> 69.9 us (0.04)
  blocking collectives: 1220 us -> 0 us
  local copies, waits for them, and re-layouts: 335 us -> 4.37 us
  starting transfers between devices: 146 us -> 0 us
  other arithmetic: 136 us -> 0 us
  Pallas kernels: 0 us -> 64.6 us
    psum x15 -> x0, blocking collectives: 1220 us -> none  [record(): local_value = lax.psum(local_value, ('gx', 'gy'))]
    while x1331 -> x0, local copies, waits for them, and re-layouts: 155 us -> none
    ppermute x64 -> x0, starting transfers between devices: 146 us -> none  [the longest x32 94.4 us: with_halo(): before = lax.ppermute(last, axis, up)]
    pallas_call x0 -> x1, Pallas kernels: none -> 64.6 us  [per_device(): pl.pallas_call(functools.partial(kernel, nx, ny, gx_size, gy_size), out_s...]
    ppermute x32 -> x0, local copies, waits for them, and re-layouts: 60.2 us -> none  [the longest x16 30.1 us: with_halo(): after = lax.ppermute(first, axis, down)]
    squeeze x42 -> x0, local copies, waits for them, and re-layouts: 52.8 us -> none  [orbital(): return (complex_field[0][:, position], complex_field[1][:, position])]
    sub x29 -> x0, other arithmetic: 27.5 us -> none  [the longest x15 21.3 us: scaled(): weight_real * complex_field[0] - weight_imag * complex_field[1]]
    scatter x14 -> x0, other arithmetic: 25.8 us -> none  [record(): return store.at[degree].set(local_value)]
  transfers between devices with their start and end apart: 64 -> 0, of which waited for: 2 -> 0; matrix products, arithmetic and copies ran while one was open for 9% -> 0% of each run, Pallas kernels for 0% -> 0%
where the time goes in v1:
time: 69.9 us; the launch traced here: 69.6 us
  Pallas kernels  64.6 us (92%)
  local copies, waits for them, and re-layouts  4.37 us (6%)
    pallas_call x1, Pallas kernels, per_device(): pl.pallas_call(functools.partial(kernel, nx, ny, gx_size, gy_size), out_s...  64.6 us
    unnamed x8, local copies, waits for them, and re-layouts  4.29 us

profile of v1, /device:TPU:1, one launch (start us, length us, event | category | flops | bytes accessed | tf_op | source)
XLA Modules:
  0.0 69.6 jit_solution(5893182978650323409)
XLA Ops:
  0.6 0.0 copy-start
  0.6 1.0 %copy-done = f32[8,4,16,256]{3,2,1,0:T(8,128)S(1)} copy-done((f32[8,4,16,256]{3,2,1,0:T(8,128)S(1)}, f32[8,4,16,256]{3,2,1,0:T(8,128)}, u32[]{:S(2)}) %copy-start) | copy-done | bytes 524312
  1.7 0.0 copy-start.1
  1.7 0.9 %copy-done.1 = s32[7,16,256]{2,1,0:T(8,128)S(1)} copy-done((s32[7,16,256]{2,1,0:T(8,128)S(1)}, s32[7,16,256]{2,1,0:T(8,128)}, u32[]{:S(2)}) %copy-start.1) | copy-done | bytes 114712
  2.6 0.0 copy-start.2
  2.6 0.7 %copy-done.2 = f32[16,256]{1,0:T(8,128)S(1)} copy-done((f32[16,256]{1,0:T(8,128)S(1)}, f32[16,256]{1,0:T(8,128)}, u32[]{:S(2)}) %copy-start.2) | copy-done | bytes 16408
  3.3 64.6 %evolve.1 = (f32[2,8,4,16,256]{4,3,2,1,0:T(8,128)S(1)}, f32[8,128]{1,0:T(8,128)S(1)}) custom-call(f32[8,4,16,256]{3,2,1,0:T(8,128)S(1)} %copy-done, s32[7,16,256]{2,1,0:T(8,128)S(1)} %copy-done.1, f32[16,256]{1,0:T(8,128)S(1)} %copy-done.2), custom_call_target="tpu_custom_call" | custom-call | tf_op jit(solution)/shard_map/evolve/pallas_call | solution.py:529
  67.9 0.1 copy.6
  68.0 0.7 copy.7
  68.7 1.0 %copy.9 = f32[2,8,4,16,256]{4,3,2,1,0:T(8,128)} copy(f32[2,8,4,16,256]{4,3,2,1,0:T(8,128)S(1)} %get-tuple-element.12) | data formatting | bytes 2097152
  (1 shorter events, 0.0 us)
Async XLA Ops:
  0.6 1.0 %copy-start = (f32[8,4,16,256]{3,2,1,0:T(8,128)S(1)}, f32[8,4,16,256]{3,2,1,0:T(8,128)}, u32[]{:S(2)}) copy-start(f32[8,4,16,256]{3,2,1,0:T(8,128)} %ang_h.1) | copy-start | bytes 1572868
  1.7 0.9 %copy-start.1 = (s32[7,16,256]{2,1,0:T(8,128)S(1)}, s32[7,16,256]{2,1,0:T(8,128)}, u32[]{:S(2)}) copy-start(s32[7,16,256]{2,1,0:T(8,128)} %flux_h.1) | copy-start | bytes 344068
  2.6 0.7 %copy-start.2 = (f32[16,256]{1,0:T(8,128)S(1)}, f32[16,256]{1,0:T(8,128)}, u32[]{:S(2)}) copy-start(f32[16,256]{1,0:T(8,128)} %coup_h.1) | copy-start | bytes 49156

commit v2 on v1

v2 whole, which is shorter than its diff:
```python
import functools
import math

import jax
import jax.numpy as jnp
from jax import lax
from jax.experimental import pallas as pl
from jax.experimental.pallas import tpu as pltpu
from jax.sharding import PartitionSpec as P

TERMS = 16
QUANTA = 64
PHASE_SPAN = 12.0

STATES = 8
ROWS = 16
COLS = 256
LANES = 128
HALO = 8
EXT = ROWS + 2 * HALO
PAD = EXT + 8
BLOCKS = EXT // 8
SIDE = 2 * HALO
TILES = 3
DEEP = (COLS + SIDE) // 16
ROW0 = 8
UNROLL = 1
A1, B2, B1, A2 = 0, 1, 2, 3
MESH = pl.DeviceIdType.MESH

T2C, T2S, T4C, T4S, T5C, T5S, CPL = range(7)


def bessel_value(degree, argument):
    running = 0.0
    for number in range(60):
        running += (
            (-1.0) ** number
            * (argument / 2.0) ** (2 * number + degree)
            / (math.factorial(number) * math.factorial(number + degree))
        )
    return running


EVEN = [(1.0 if m == 0 else 2.0) * (-1.0) ** m * bessel_value(2 * m, PHASE_SPAN) for m in range(TERMS // 2)]
ODD = [-2.0 * (-1.0) ** m * bessel_value(2 * m + 1, PHASE_SPAN) for m in range(TERMS // 2)]

SIN_COEF = [(-1.0) ** n * math.pi ** (2 * n + 1) / math.factorial(2 * n + 1) for n in range(6)]
COS_COEF = [(-1.0) ** n * math.pi ** (2 * n) / math.factorial(2 * n) for n in range(7)]


def turn(f):
    r = f - jnp.floor(f + 0.5)
    q = r * r
    s = SIN_COEF[-1]
    for value in reversed(SIN_COEF[:-1]):
        s = s * q + value
    s = s * r
    c = COS_COEF[-1]
    for value in reversed(COS_COEF[:-1]):
        c = c * q + value
    return 1.0 - 2.0 * s * s, 2.0 * s * c


def rot(c, s, v):
    return c * v[0] - s * v[1], s * v[0] + c * v[1]


def rot_back(c, s, v):
    return c * v[0] + s * v[1], c * v[1] - s * v[0]


def add(*pairs):
    re, im = pairs[0]
    for pair in pairs[1:]:
        re, im = re + pair[0], im + pair[1]
    return re, im


def kernel(
    nx, ny, gx_size, gy_size,
    ang_h, flux_h, coup_h, evo_h, mom_ref,
    ang, fli, flf, u, hist, ft, phf, af, px, spread_m, perm_m, back_m, gauge, chi, vel, tf, tl, outv, mom, pack, got, msg_1, msg_2, in_1, in_2,
    load_sem, out_sem, xs_sem, xr_sem, ps_sem, pr_sem, s1_sem, r1_sem, s2_sem, r2_sem,
):
    gx, gy = lax.axis_index("gx"), lax.axis_index("gy")
    group_1, group_2 = gx_size // 2, 2 * gy_size
    half, place_1 = gx // group_1, lax.rem(gx, group_1)
    place_2 = half * gy_size + gy

    def near(dx, dy):
        return (lax.rem(gx + dx + gx_size, gx_size), lax.rem(gy + dy + gy_size, gy_size))

    def peer_1(other):
        return (half * group_1 + other, gy)

    def peer_2(other):
        return (other // gy_size * group_1 + place_1, lax.rem(other, gy_size))

    lane = lax.broadcasted_iota(jnp.int32, (STATES, LANES), 1)
    sub = lax.broadcasted_iota(jnp.int32, (8, LANES), 0)
    first_lane, last_lane = lane == 0, lane == LANES - 1
    zero = jnp.zeros((STATES, LANES), jnp.float32)

    loads = []
    for t in range(2):
        span = pl.ds(t * LANES, LANES)
        own = pl.ds(HALO, ROWS)
        loads.append(pltpu.make_async_copy(flux_h.at[:, :, span], fli.at[t, :, own, :], load_sem.at[t, 0]))
        loads.append(pltpu.make_async_copy(coup_h.at[:, span], flf.at[t, pl.ds(7 * PAD + HALO, ROWS), :], load_sem.at[t, 1]))
        loads.append(pltpu.make_async_copy(ang_h.at[:, :, :, span], ang.at[t, :, :, own, :], load_sem.at[t, 2]))
    for copy in loads:
        copy.start()

    barrier = pltpu.get_barrier_semaphore()

    def greet(peer, me, size):
        def one(d, carry):
            pl.semaphore_signal(barrier, inc=1, device_id=peer(lax.rem(me + d, size)), device_id_type=MESH)
            return carry

        lax.fori_loop(1, size, one, 0)

    for dx in (-1, 0, 1):
        for dy in (-1, 0, 1):
            if dx or dy:
                pl.semaphore_signal(barrier, inc=1, device_id=near(dx, dy), device_id_type=MESH)
    greet(peer_1, place_1, group_1)
    greet(peer_2, place_2, group_2)

    for t in range(TILES):
        for plane in range(8):
            flf[t, pl.ds(plane * PAD + EXT, 8), :] = zero

    for copy in loads:
        copy.wait()

    def flux_to_float(t, start, count):
        for plane in range(7):
            flf[t, pl.ds(plane * PAD + start, count), :] = fli[t, plane, pl.ds(start, count), :].astype(jnp.float32)

    for t in range(2):
        flux_to_float(t, HALO, ROWS)

    group = lane // HALO

    def packed(side, value_of):
        out = zero
        for r in range(8):
            value = value_of(r)
            move = (SIDE * r + (SIDE if side == 0 else 0)) % LANES
            if move:
                value = pltpu.roll(value, move, 1)
            out = jnp.where(group == 2 * r + 1 - side, value, out)
        return out

    def pack_angles(orb, carry):
        for side in range(2):
            for block in range(2):
                rows = pl.ds(HALO + 8 * block, 8)
                pack[side, block, orb] = packed(side, lambda r: ang[1 - side, r, orb, rows, :])
        return carry

    lax.fori_loop(0, 4, pack_angles, 0)
    for side in range(2):
        for block in range(2):
            pack[side, block, 4] = packed(side, lambda r: flf[1 - side, pl.ds(r * PAD + HALO + 8 * block, 8), :])

    pl.semaphore_wait(barrier, 8 + group_1 - 1 + group_2 - 1)

    row_copies = []
    for side, dx in ((0, 1), (1, -1)):
        src_rows = pl.ds(ROWS - HALO, HALO) if side == 0 else pl.ds(0, HALO)
        low = 0 if side == 0 else HALO + ROWS
        for t in range(2):
            span = pl.ds(t * LANES, LANES)
            for what, (src, dst) in enumerate(
                (
                    (flux_h.at[:, src_rows, span], fli.at[t, :, pl.ds(low, HALO), :]),
                    (coup_h.at[src_rows, span], flf.at[t, pl.ds(7 * PAD + low, HALO), :]),
                    (ang_h.at[:, :, src_rows, span], ang.at[t, :, :, pl.ds(low, HALO), :]),
                )
            ):
                row_copies.append(
                    (
                        what,
                        pltpu.make_async_remote_copy(
                            src_ref=src,
                            dst_ref=dst,
                            send_sem=xs_sem.at[side, t, what],
                            recv_sem=xr_sem.at[side, t, what],
                            device_id=near(dx, 0),
                            device_id_type=MESH,
                        ),
                    )
                )
    pack_copies = []
    for side, dy in ((0, 1), (1, -1)):
        for dx, src, dst in (
            (0, pack.at[side], got.at[side, pl.ds(1, 2)]),
            (1, pack.at[side, 1], got.at[side, 0]),
            (-1, pack.at[side, 0], got.at[side, 3]),
        ):
            pack_copies.append(
                pltpu.make_async_remote_copy(
                    src_ref=src,
                    dst_ref=dst,
                    send_sem=ps_sem.at[side, 1 - dx],
                    recv_sem=pr_sem.at[side, 1 - dx],
                    device_id=near(dx, dy),
                    device_id_type=MESH,
                )
            )
    for what, copy in row_copies:
        if what < 2:
            copy.start()
    for copy in pack_copies:
        copy.start()
    for what, copy in row_copies:
        if what == 2:
            copy.start()

    def flux_of(t, plane, start, count=8):
        return flf[t, pl.ds(plane * PAD + start, count), :]

    def wrapped(value):
        return value - QUANTA * jnp.floor(value * (1.0 / QUANTA))

    def cell_phases(t, start, carry):
        if start < HALO:
            run = flux_of(t, 1, start + 1) - flux_of(t, 0, start + 1)
            for reach in (1, 2, 4):
                run = run + jnp.where(sub < 8 - reach, pltpu.roll(run, 8 - reach, 0), 0.0)
        else:
            run = flux_of(t, 0, start) - flux_of(t, 1, start)
            if start == HALO:
                run = jnp.where(sub == 0, 0.0, run)
            for reach in (1, 2, 4):
                run = run + jnp.where(sub >= reach, pltpu.roll(run, reach, 0), 0.0)
            if carry is not None:
                run = run + carry
        run = wrapped(run)
        chi[t, pl.ds(start, 8), :] = run
        th0, th3, th6 = (flux_of(t, plane, start) for plane in (0, 3, 6))
        rows = pl.ds(start, 8)
        span = pl.ds(t * LANES, LANES)
        px[A1, rows, span] = wrapped(run - th0 + QUANTA // 2)
        px[B2, rows, span] = wrapped(th6 + th3 + run + QUANTA // 2)
        px[B1, rows, span] = run
        px[A2, rows, span] = wrapped(th6 + run)
        return jnp.broadcast_to(run[7:8, :], (8, LANES))

    carries = []
    for t in range(2):
        carry = None
        for start in (HALO, HALO + 8):
            carry = cell_phases(t, start, carry)
            for orb in range(4):
                c, s = turn(px[orb, pl.ds(start, 8), pl.ds(t * LANES, LANES)] * (1.0 / QUANTA))
                if orb in (A1, A2):
                    c, s = 0.5 * c, 0.5 * s
                gauge[orb, 0, t, pl.ds(start - HALO, 8), :] = c
                gauge[orb, 1, t, pl.ds(start - HALO, 8), :] = s
        carries.append(carry)

    def row_place(shape):
        at = lax.broadcasted_iota(jnp.int32, shape, 0)
        return jnp.where(at < COLS + HALO, at + HALO, jnp.where(at < COLS + SIDE, at - COLS - HALO, -1))

    def one_hot(here):
        return jnp.where(here, 1.0, 0.0).astype(jnp.bfloat16)

    at_row = row_place((TILES * LANES, LANES))
    at_lane = lax.rem(lax.broadcasted_iota(jnp.int32, (TILES * LANES, LANES), 1), SIDE) * DEEP

    def make_spread(y, carry):
        spread_m[:, pl.ds(pl.multiple_of(y * LANES, LANES), LANES)] = one_hot(at_row == at_lane + y)
        return carry

    lax.fori_loop(0, DEEP, make_spread, 0)
    wide = lax.broadcasted_iota(jnp.int32, (COLS, TILES * LANES), 1)
    tall = lax.broadcasted_iota(jnp.int32, (COLS, TILES * LANES), 0)
    perm_m[...] = one_hot((tall + HALO == lax.rem(wide, SIDE) * DEEP + wide // SIDE) & (wide < SIDE * DEEP))
    wide = lax.broadcasted_iota(jnp.int32, (TILES * LANES, COLS), 1)
    tall = lax.broadcasted_iota(jnp.int32, (TILES * LANES, COLS), 0)
    back_m[...] = one_hot((wide + HALO == lax.rem(tall, SIDE) * DEEP + tall // SIDE) & (tall < SIDE * DEEP))

    def moved(value, matrix):
        parts = []
        for _ in range(3):
            parts.append(value.astype(jnp.bfloat16))
            value = value - parts[-1].astype(jnp.float32)
        out = jnp.dot(jnp.concatenate(parts, axis=0), matrix, preferred_element_type=jnp.float32)
        size = value.shape[0]
        return out[:size] + out[size : 2 * size] + out[2 * size :]

    lane_group = lane // SIDE

    def exchanged(values):
        values = list(values)
        for s in (1, 2, 4):
            keep = (lane_group // s) % 2 == 0
            for i in range(8):
                if not i & s:
                    one, two = values[i], values[i | s]
                    values[i] = jnp.where(keep, one, pltpu.roll(two, SIDE * s, 1))
                    values[i | s] = jnp.where(keep, pltpu.roll(one, LANES - SIDE * s, 1), two)
        return values

    def spread_angles(blocks):
        def spread_orb(orb, carry):
            value = jnp.concatenate(
                [
                    jnp.concatenate(
                        [ang[t, :, orb, pl.ds(8 * block, 8), :].reshape(STATES * 8, LANES) for t in range(2)], axis=1
                    )
                    for block in blocks
                ],
                axis=0,
            )
            out = moved(value, perm_m[...])
            for which, block in enumerate(blocks):
                parts = [
                    [
                        out[64 * which + 8 * r : 64 * which + 8 * r + 8, LANES * t : LANES * t + LANES]
                        for r in range(8)
                    ]
                    for t in range(TILES)
                ]
                deep = exchanged(parts[0]) + exchanged(parts[1])
                last = parts[2][0]
                for r in range(1, 8):
                    last = jnp.where(lane_group == r, pltpu.roll(parts[2][r], SIDE * r, 1), last)
                for y, value in enumerate(deep + [last]):
                    af[orb, y, pl.ds(8 * block, 8), :] = value
            return carry

        lax.fori_loop(0, 4, spread_orb, 0)

    spread_angles((1, 2))

    for what, copy in row_copies:
        if what < 2:
            copy.wait()
    for t in range(2):
        for start in (0, HALO + ROWS):
            flux_to_float(t, start, HALO)
            cell_phases(t, start, carries[t])
    for copy in pack_copies:
        copy.wait()

    beside = lax.rem(lane, SIDE)

    def unpack(what, block):
        return jnp.where(beside < HALO, got[1, block, what], got[0, block, what])

    for block in range(BLOCKS):
        values = unpack(4, block)
        for which in range(8):
            move = (LANES - SIDE * which) % LANES
            flf[2, pl.ds(which * PAD + 8 * block, 8), :] = pltpu.roll(values, move, 1) if move else values
    carry = None
    for start in (HALO, HALO + 8, HALO + ROWS, 0):
        carry = cell_phases(2, start, carry)

    def right(values):
        rolled = [pltpu.roll(value, 1, 1) for value in values]
        edges = [pltpu.roll(values[2], LANES - SIDE + 1, 1), rolled[0], rolled[1]]
        return [jnp.where(first_lane, edges[t], rolled[t]) for t in range(TILES)]

    def left(values):
        rolled = [pltpu.roll(value, LANES - 1, 1) for value in values]
        edge = pltpu.roll(values[0], SIDE - 1, 1)
        return [
            jnp.where(last_lane, rolled[1], rolled[0]),
            jnp.where(last_lane, rolled[2], rolled[1]),
            jnp.where(lane == SIDE - 1, edge, rolled[2]),
        ]

    for start in range(0, EXT, 8):
        rows = pl.ds(start, 8)
        th = [[flux_of(t, plane, start) for plane in range(8)] for t in range(TILES)]
        cell = [chi[t, rows, :] for t in range(TILES)]
        cell_left, cell_right = right(cell), left(cell)
        far = left([th[t][6] + th[t][3] for t in range(TILES)])
        for t in range(TILES):
            span = pl.ds(t * LANES, LANES)
            below = [flux_of(t, plane, start + 1) for plane in (6, 3, 1, 0)]
            px[4, rows, span] = wrapped(th[t][2] - th[t][0] + cell[t] - cell_left[t])
            px[5, rows, span] = wrapped(th[t][4] + th[t][6] - below[0] - below[1] + below[2] - below[3])
            px[6, rows, span] = wrapped(th[t][5] + th[t][6] - far[t] + cell[t] - cell_right[t])
            rest = th[t][7]
            for part in range(3):
                head = rest.astype(jnp.bfloat16).astype(jnp.float32)
                px[7 + part, rows, span] = head
                rest = rest - head

    planes = px[...].reshape(10 * EXT, TILES * LANES).astype(jnp.bfloat16)
    lane_place = lax.rem(lane, SIDE) * DEEP
    sub_i = gx * ROWS - HALO + sub

    def cell_inside(y, block):
        j = gy * COLS - HALO + lane_place + y
        i = sub_i + 8 * block
        return (j >= 0) & (j < ny) & (i >= 0) & (i < nx)

    def make_tables(y, carry):
        out = jnp.dot(
            planes,
            spread_m[:, pl.ds(pl.multiple_of(y * LANES, LANES), LANES)],
            preferred_element_type=jnp.float32,
        )
        place = lane_place + y
        j = gy * COLS - HALO + place
        for block in range(BLOCKS):
            rows = pl.ds(ROW0 + 8 * block, 8)
            part = [out[which * EXT + 8 * block : which * EXT + 8 * block + 8, :] for which in range(10)]
            for orb in range(4):
                phf[orb, y, pl.ds(8 * block, 8), :] = part[orb] * (1.0 / QUANTA)
            here = cell_inside(y, block)
            for which, good in (
                (T2C, here & (j >= 1) & (place >= 1)),
                (T4C, here & (sub_i + 8 * block + 1 < nx)),
                (T5C, here & (j + 1 < ny) & (place < SIDE * DEEP - 1)),
            ):
                c, s = turn(part[4 + which // 2] * (1.0 / QUANTA))
                ft[which, y + 1, rows, :] = jnp.where(good, c, 0.0)
                ft[which + 1, y + 1, rows, :] = jnp.where(good, s, 0.0)
            ft[CPL, y + 1, rows, :] = jnp.where(here, part[7] + part[8] + part[9], 0.0)
        return carry

    lax.fori_loop(0, DEEP, make_tables, 0)
    for block in range(BLOCKS):
        rows = pl.ds(ROW0 + 8 * block, 8)
        for which in (T2C, T2S):
            ft[which, DEEP + 1, rows, :] = pltpu.roll(ft[which, 1, rows, :], LANES - 1, 1)
        for which in (T5C, T5S):
            ft[which, 0, rows, :] = pltpu.roll(ft[which, DEEP, rows, :], 1, 1)

    def start_values(blocks):
        def start_one(y, carry):
            place = lane_place + y
            beyond = (place < HALO) | (place >= COLS + HALO)
            move = jnp.where(y <= HALO, LANES - HALO - y, SIDE + HALO - y)
            for block in blocks:
                here = cell_inside(y, block)
                rows = pl.ds(8 * block, 8)
                for orb in range(4):
                    angle = jnp.where(beyond, pltpu.roll(unpack(orb, block), move, 1), af[orb, y, rows, :])
                    c, s = turn(angle * (0.5 / math.pi) + phf[orb, y, rows, :])
                    size = 2.0 if orb in (A1, A2) else 1.0
                    u[0, 2 * orb, y + 1, pl.ds(ROW0 + 8 * block, 8), :] = jnp.where(here, size * c, 0.0)
                    u[0, 2 * orb + 1, y + 1, pl.ds(ROW0 + 8 * block, 8), :] = jnp.where(here, size * s, 0.0)
            return carry

        lax.fori_loop(0, DEEP, start_one, 0)

    start_values((1, 2))
    for what, copy in row_copies:
        if what == 2:
            copy.wait()
    spread_angles((0, 3))
    start_values((0, 3))

    def site(buf, orb, y, row):
        rows = pl.ds(ROW0 + row, 8)
        return u[buf, 2 * orb, y + 1, rows, :], u[buf, 2 * orb + 1, y + 1, rows, :]

    def table(which, y, row):
        rows = pl.ds(ROW0 + row, 8)
        return ft[which, y + 1, rows, :], ft[which + 1, y + 1, rows, :]

    def join(buf, row):
        rows = pl.ds(ROW0 + row, 8)
        for part in range(2):
            for orb in (B1, A2):
                u[buf, 2 * orb + part, 0, rows, :] = pltpu.roll(u[buf, 2 * orb + part, DEEP, rows, :], 1, 1)
            for orb in (A1, B2):
                u[buf, 2 * orb + part, DEEP + 1, rows, :] = pltpu.roll(u[buf, 2 * orb + part, 1, rows, :], LANES - 1, 1)

    for block in range(BLOCKS):
        join(0, 8 * block)

    def velocity(y, carry):
        place = lane_place + y
        own = jnp.where((place >= HALO) & (place < COLS + HALO), 0.5, 0.0)
        for block in range(2):
            row = HALO + 8 * block
            v = [None] * 4
            v[A1] = [own * part for part in site(0, B1, y, row - 1)]
            v[B1] = [-own * part for part in site(0, A1, y, row + 1)]
            v[A2] = [-own * part for part in rot(*table(T4C, y, row), site(0, B2, y, row + 1))]
            v[B2] = [own * part for part in rot_back(*table(T4C, y, row - 1), site(0, A2, y, row - 1))]
            for orb in range(4):
                for part in range(2):
                    vel[y, block, 2 * orb + part] = v[orb][part]
        return carry

    lax.fori_loop(0, DEEP, velocity, 0)

    def step_at(src, dst, y, row, first):
        a1, b2, b1, a2 = (site(src, orb, y, row) for orb in range(4))
        hop = ft[CPL, y + 1, pl.ds(ROW0 + row, 8), :]
        new = [None] * 4
        new[A1] = add(b1, site(src, B1, y, row - 1), rot(*table(T2C, y, row), site(src, B1, y - 1, row)))
        new[B1] = add(
            a1,
            site(src, A1, y, row + 1),
            rot_back(*table(T2C, y + 1, row), site(src, A1, y + 1, row)),
            (hop * a2[0], hop * a2[1]),
        )
        new[A2] = add(
            b2,
            rot(*table(T4C, y, row), site(src, B2, y, row + 1)),
            rot(*table(T5C, y, row), site(src, B2, y + 1, row)),
            (hop * b1[0], hop * b1[1]),
        )
        new[B2] = add(
            a2,
            rot_back(*table(T4C, y, row - 1), site(src, A2, y, row - 1)),
            rot_back(*table(T5C, y - 1, row), site(src, A2, y - 1, row)),
        )
        for orb in range(4):
            size = 1.0 if orb in (A1, A2) else 0.25
            for part in range(2):
                value = new[orb][part]
                rows = pl.ds(ROW0 + row, 8)
                if first:
                    value = (0.5 * size) * value
                else:
                    value = (value if size == 1.0 else size * value) - u[dst, 2 * orb + part, y + 1, rows, :]
                u[dst, 2 * orb + part, y + 1, rows, :] = value

    def step(src, dst, rows, first=False):
        def step_one(y, carry):
            for row in rows:
                step_at(src, dst, y, row, first)
            return carry

        lax.fori_loop(0, DEEP, step_one, 0, unroll=UNROLL)
        for row in rows:
            join(dst, row)

        @pl.when(gx == 0)
        def _():
            for orb in (B1, A2):
                for part in range(2):
                    u[dst, 2 * orb + part, :, pl.ds(ROW0 + HALO - 1, 1), :] = jnp.zeros((DEEP + 2, 1, LANES), jnp.float32)

        @pl.when(gx == gx_size - 1)
        def _():
            for orb in (A1, B2):
                for part in range(2):
                    u[dst, 2 * orb + part, :, pl.ds(ROW0 + HALO + ROWS, 1), :] = jnp.zeros((DEEP + 2, 1, LANES), jnp.float32)

    def gather(k):
        def gather_one(y, sums):
            sums = list(sums)
            for block in range(2):
                for orb in range(4):
                    vr, vi = vel[y, block, 2 * orb], vel[y, block, 2 * orb + 1]
                    for which in range(2):
                        ur, ui = site(which, orb, y, HALO + 8 * block)
                        hist[k + which, y, block, 2 * orb], hist[k + which, y, block, 2 * orb + 1] = ur, ui
                        sums[2 * which] += vr * ur + vi * ui
                        sums[2 * which + 1] += vr * ui - vi * ur
            return tuple(sums)

        sums = lax.fori_loop(0, DEEP, gather_one, (zero,) * 4)
        for which in range(4):
            mom[2 * k + which] = sums[which]

    far_rows, mid_rows, own_rows = (0, 8, 16, 24), (4, 12, 20), (8, 16)
    step(0, 1, far_rows, first=True)
    gather(0)

    def early(m, carry):
        step(1, 0, far_rows)
        step(0, 1, far_rows)
        gather(2 * m)
        return carry

    def late(m, carry):
        step(1, 0, mid_rows)
        step(0, 1, mid_rows)
        gather(2 * m)
        return carry

    lax.fori_loop(1, 4, early, 0)
    lax.fori_loop(4, TERMS // 2 - 1, late, 0)
    step(1, 0, mid_rows)
    step(0, 1, own_rows)
    gather(TERMS - 2)

    sums = []
    for part in (1, 0):
        for k in range(TERMS):
            sums.append(jnp.sum(mom[2 * k + part], axis=0, keepdims=True))
    state = lax.broadcasted_iota(jnp.int32, (STATES, LANES), 0)
    ones = jnp.where(lane_group == state, 1.0, 0.0)
    local = lax.dot_general(
        ones,
        jnp.concatenate(sums + [jnp.zeros((LANES - 2 * TERMS, LANES), jnp.float32)], axis=0),
        (((1,), (1,)), ((), ())),
        precision=lax.Precision.HIGHEST,
        preferred_element_type=jnp.float32,
    )
    local = jnp.where(lane < TERMS, local, -local) * (1.0 / math.sqrt(4.0 * nx * ny))
    wide = 2 * TERMS
    spread_out = zero
    for q in range(4):
        value = pltpu.roll(local, wide * q, 1) if q else local
        spread_out = jnp.where((lax.rem(sub, 4) == q) & (lane // wide == q), value, spread_out)
    folded = jnp.concatenate(
        [jnp.sum(spread_out[:4], axis=0, keepdims=True), jnp.sum(spread_out[4:], axis=0, keepdims=True)], axis=0
    )

    def spread(value, msg, slots, me, size, peer, send_sem, recv_sem):
        msg[...] = value
        slots[me] = value

        def copy_to(other, slot, d):
            return pltpu.make_async_remote_copy(
                src_ref=msg,
                dst_ref=slots.at[slot],
                send_sem=send_sem.at[d],
                recv_sem=recv_sem.at[slot],
                device_id=peer(other),
                device_id_type=MESH,
            )

        def send(d, carry):
            copy_to(lax.rem(me + d, size), me, d).start()
            return carry

        def finish(d, carry):
            other = lax.rem(me + d, size)
            copy_to(other, me, d).wait_send()
            copy_to(other, other, d).wait_recv()
            return carry

        lax.fori_loop(1, size, send, 0)
        return lambda: lax.fori_loop(1, size, finish, 0)

    def total(slots, size):
        value = slots[0]
        for at in range(1, size):
            value = value + slots[at]
        return value

    def out_copy(orb):
        return pltpu.make_async_copy(outv.at[:, :, orb], evo_h.at[:, :, orb], out_sem.at[orb])

    def evolve(orb, carry):
        def evolve_one(y, carry):
            for block in range(2):
                re, im = zero, zero
                for m in range(TERMS // 2):
                    a, b = ((hist[2 * m + n, y, block, 2 * orb], hist[2 * m + n, y, block, 2 * orb + 1]) for n in range(2))
                    re = re + (EVEN[m] * a[0] - ODD[m] * b[1])
                    im = im + (EVEN[m] * a[1] + ODD[m] * b[0])
                tf[block, y], tf[2 + block, y] = re, im
            return carry

        lax.fori_loop(0, DEEP, evolve_one, 0)

        def back(which, carry):
            tiles = [exchanged([tf[which, 8 * t + i] for i in range(8)]) for t in range(2)]
            last = tf[which, DEEP - 1]
            tiles.append([pltpu.roll(last, LANES - SIDE * r, 1) if r else last for r in range(8)])
            for t in range(TILES):
                for r in range(8):
                    tl[which, pl.ds(8 * r, 8), pl.ds(LANES * t, LANES)] = tiles[t][r]
            return carry

        lax.fori_loop(0, 4, back, 0)
        out = moved(tl[...].reshape(4 * 64, TILES * LANES), back_m[...])
        for block in range(2):
            rows = pl.ds(8 * block, 8)
            c = jnp.concatenate([gauge[orb, 0, t, rows, :] for t in range(2)], axis=1)
            s = jnp.concatenate([gauge[orb, 1, t, rows, :] for t in range(2)], axis=1)
            for r in range(8):
                at = 64 * block + 8 * r
                v = rot_back(c, s, (out[at : at + 8, :], out[128 + at : 128 + at + 8, :]))
                outv[0, r, orb, rows, :], outv[1, r, orb, rows, :] = v
        out_copy(orb).start()
        return carry

    finish_1 = spread(folded, msg_1, in_1, place_1, group_1, peer_1, s1_sem, r1_sem)
    lax.fori_loop(0, 2, evolve, 0)
    finish_1()
    finish_2 = spread(total(in_1, group_1), msg_2, in_2, place_2, group_2, peer_2, s2_sem, r2_sem)
    lax.fori_loop(2, 4, evolve, 0)
    finish_2()
    folded = total(in_2, group_2)
    rows = jnp.where(sub < 4, folded[0:1, :], folded[1:2, :])
    result = rows
    for q in range(1, 4):
        result = jnp.where(lax.rem(sub, 4) == q, pltpu.roll(rows, LANES - wide * q, 1), result)
    mom_ref[0] = result[:, :TERMS]
    mom_ref[1] = pltpu.roll(result, LANES - TERMS, 1)[:, :TERMS]
    for orb in range(4):
        out_copy(orb).wait()


def per_device(nx, ny, gx_size, gy_size, angles, bond_flux, coupling):
    f32 = jnp.float32
    tile = (STATES, LANES)
    group_1, group_2 = gx_size // 2, 2 * gy_size
    evolved, moments = pl.pallas_call(
        functools.partial(kernel, nx, ny, gx_size, gy_size),
        out_shape=(
            jax.ShapeDtypeStruct((2, STATES, 4, ROWS, COLS), f32),
            jax.ShapeDtypeStruct((2, STATES, TERMS), f32),
        ),
        in_specs=[pl.BlockSpec(memory_space=pl.ANY)] * 3,
        out_specs=(pl.BlockSpec(memory_space=pl.ANY), pl.BlockSpec(memory_space=pltpu.VMEM)),
        scratch_shapes=[
            pltpu.VMEM((2, STATES, 4, EXT, LANES), f32),
            pltpu.VMEM((2, 7, EXT, LANES), jnp.int32),
            pltpu.VMEM((TILES, 8 * PAD, LANES), f32),
            pltpu.VMEM((2, 8, DEEP + 2, EXT + 2 * ROW0, LANES), f32),
            pltpu.VMEM((TERMS, DEEP, 2, 8) + tile, f32),
            pltpu.VMEM((7, DEEP + 2, EXT + 2 * ROW0, LANES), f32),
            pltpu.VMEM((4, DEEP, EXT, LANES), f32),
            pltpu.VMEM((4, DEEP, EXT, LANES), f32),
            pltpu.VMEM((10, EXT, TILES * LANES), f32),
            pltpu.VMEM((TILES * LANES, DEEP * LANES), jnp.bfloat16),
            pltpu.VMEM((COLS, TILES * LANES), jnp.bfloat16),
            pltpu.VMEM((TILES * LANES, COLS), jnp.bfloat16),
            pltpu.VMEM((4, 2, 2, ROWS, LANES), f32),
            pltpu.VMEM((TILES, EXT, LANES), f32),
            pltpu.VMEM((DEEP, 2, 8) + tile, f32),
            pltpu.VMEM((4, DEEP) + tile, f32),
            pltpu.VMEM((4, 64, TILES * LANES), f32),
            pltpu.VMEM((2, STATES, 4, ROWS, COLS), f32),
            pltpu.VMEM((2 * TERMS,) + tile, f32),
            pltpu.VMEM((2, 2, 5) + tile, f32),
            pltpu.VMEM((2, BLOCKS, 5) + tile, f32),
            pltpu.VMEM((2, LANES), f32),
            pltpu.VMEM((2, LANES), f32),
            pltpu.VMEM((group_1, 2, LANES), f32),
            pltpu.VMEM((group_2, 2, LANES), f32),
            pltpu.SemaphoreType.DMA((2, 3)),
            pltpu.SemaphoreType.DMA((4,)),
            pltpu.SemaphoreType.DMA((2, 2, 3)),
            pltpu.SemaphoreType.DMA((2, 2, 3)),
            pltpu.SemaphoreType.DMA((2, 3)),
            pltpu.SemaphoreType.DMA((2, 3)),
            pltpu.SemaphoreType.DMA((group_1,)),
            pltpu.SemaphoreType.DMA((group_1,)),
            pltpu.SemaphoreType.DMA((group_2,)),
            pltpu.SemaphoreType.DMA((group_2,)),
        ],
        compiler_params=pltpu.CompilerParams(
            collective_id=0, has_side_effects=True, vmem_limit_bytes=60 * 2**20
        ),
        name="evolve",
    )(angles, bond_flux, coupling)
    return evolved, jnp.transpose(moments, (2, 0, 1))


def solution(mesh):
    in_specs = (P(None, None, "gx", "gy"), P(None, "gx", "gy"), P("gx", "gy"))
    out_specs = (P(None, None, None, "gx", "gy"), P())
    gx_size, gy_size = mesh.shape["gx"], mesh.shape["gy"]
    return jax.shard_map(
        functools.partial(per_device, gx_size * ROWS, gy_size * COLS, gx_size, gy_size),
        mesh=mesh,
        in_specs=in_specs,
        out_specs=out_specs,
        check_vma=False,
    )
```

time: 69.9 us -> 60.7 us (0.87)
  Pallas kernels: 64.6 us -> 57 us
  local copies, waits for them, and re-layouts: 4.37 us -> 2.9 us
    pallas_call x1, Pallas kernels: 64.6 us -> 57 us  [per_device(): pl.pallas_call(functools.partial(kernel, nx, ny, gx_size, gy_size), out_s...]
    unnamed x8 -> x4, local copies, waits for them, and re-layouts: 4.29 us -> 2.9 us
where the time goes in v2:
time: 60.7 us; the launch traced here: 60.6 us
  Pallas kernels  57 us (94%)
  local copies, waits for them, and re-layouts  2.9 us (5%)
  between operations  0.65 us (1%)
    pallas_call x1, Pallas kernels, per_device(): pl.pallas_call(functools.partial(kernel, nx, ny, gx_size, gy_size), out_s...  57 us
    unnamed x4, local copies, waits for them, and re-layouts  2.9 us

profile of v2, /device:TPU:1, one launch (start us, length us, event | category | flops | bytes accessed | tf_op | source)
XLA Modules:
  0.0 60.6 jit_solution(1383634925922288897)
XLA Ops:
  0.6 57.0 %evolve.1 = (f32[2,8,4,16,256]{4,3,2,1,0:T(8,128)}, f32[2,8,16]{2,1,0:T(8,128)}) custom-call(f32[8,4,16,256]{3,2,1,0:T(8,128)} %ang_h.1, s32[7,16,256]{2,1,0:T(8,128)} %flux_h.1, f32[16,256]{1,0:T(8,128)} %coup_h.1), custom_call_target="tpu_custom_call" | custom-call | tf_op jit(solution)/shard_map/evolve/pallas_call | solution.py:710
  57.7 0.0 copy-start
  57.7 2.3 %copy.7 = f32[2,8,4,16,256]{4,3,2,1,0:T(8,128)} copy(f32[2,8,4,16,256]{4,3,2,1,0:T(8,128)} %get-tuple-element.8) | data formatting | bytes 2097152
  60.0 0.0 copy-done
  60.0 0.6 copy.8
Async XLA Ops:
  57.7 2.3 %copy-start = (f32[2,8,16]{2,1,0:T(8,128)S(1)}, f32[2,8,16]{2,1,0:T(8,128)}, u32[]{:S(2)}) copy-start(f32[2,8,16]{2,1,0:T(8,128)} %get-tuple-element.5) | copy-start | bytes 3076

commit v3 on v2

--- a/solution.py
+++ b/solution.py
@@ -3,6 +3,7 @@
 
 import jax
 import jax.numpy as jnp
+import numpy as np
 from jax import lax
 from jax.experimental import pallas as pl
 from jax.experimental.pallas import tpu as pltpu
@@ -45,21 +46,30 @@
 EVEN = [(1.0 if m == 0 else 2.0) * (-1.0) ** m * bessel_value(2 * m, PHASE_SPAN) for m in range(TERMS // 2)]
 ODD = [-2.0 * (-1.0) ** m * bessel_value(2 * m + 1, PHASE_SPAN) for m in range(TERMS // 2)]
 
-SIN_COEF = [(-1.0) ** n * math.pi ** (2 * n + 1) / math.factorial(2 * n + 1) for n in range(6)]
-COS_COEF = [(-1.0) ** n * math.pi ** (2 * n) / math.factorial(2 * n) for n in range(7)]
-
-
-def turn(f):
-    r = f - jnp.floor(f + 0.5)
-    q = r * r
-    s = SIN_COEF[-1]
-    for value in reversed(SIN_COEF[:-1]):
-        s = s * q + value
-    s = s * r
-    c = COS_COEF[-1]
-    for value in reversed(COS_COEF[:-1]):
-        c = c * q + value
-    return 1.0 - 2.0 * s * s, 2.0 * s * c
+def fitted(function, terms):
+    nodes = 0.125 - 0.125 * np.cos(math.pi * (np.arange(40) + 0.5) / 40)
+    fit = np.polynomial.chebyshev.Chebyshev.fit(nodes, function(np.sqrt(nodes)), terms - 1, domain=[0.0, 0.25])
+    return [float(value) for value in fit.convert(kind=np.polynomial.Polynomial).coef]
+
+
+SIN_COEF = fitted(lambda r: np.sin(math.pi * r) / r, 5)
+COS_COEF = fitted(lambda r: np.cos(math.pi * r), 6)
+
+
+def small_turn(p, unit=1, size=1.0):
+    q = p * p
+    s, c = SIN_COEF[-1] / unit ** (2 * len(SIN_COEF) - 1), COS_COEF[-1] / unit ** (2 * len(COS_COEF) - 2)
+    for power in reversed(range(len(SIN_COEF) - 1)):
+        s = s * q + SIN_COEF[power] / unit ** (2 * power + 1)
+    for power in reversed(range(len(COS_COEF) - 1)):
+        c = c * q + COS_COEF[power] / unit ** (2 * power)
+    s = s * p
+    twice = (2.0 * size) * s
+    return size - twice * s, twice * c
+
+
+def turn(f, size=1.0):
+    return small_turn(f - jnp.floor(f + 0.5), 1, size)
 
 
 def rot(c, s, v):
@@ -224,7 +234,7 @@
         return flf[t, pl.ds(plane * PAD + start, count), :]
 
     def wrapped(value):
-        return value - QUANTA * jnp.floor(value * (1.0 / QUANTA))
+        return value - QUANTA * jnp.floor(value * (1.0 / QUANTA) + 0.5)
 
     def cell_phases(t, start, carry):
         if start < HALO:
@@ -256,7 +266,7 @@
         for start in (HALO, HALO + 8):
             carry = cell_phases(t, start, carry)
             for orb in range(4):
-                c, s = turn(px[orb, pl.ds(start, 8), pl.ds(t * LANES, LANES)] * (1.0 / QUANTA))
+                c, s = small_turn(px[orb, pl.ds(start, 8), pl.ds(t * LANES, LANES)], QUANTA)
                 if orb in (A1, A2):
                     c, s = 0.5 * c, 0.5 * s
                 gauge[orb, 0, t, pl.ds(start - HALO, 8), :] = c
@@ -277,7 +287,7 @@
         spread_m[:, pl.ds(pl.multiple_of(y * LANES, LANES), LANES)] = one_hot(at_row == at_lane + y)
         return carry
 
-    lax.fori_loop(0, DEEP, make_spread, 0)
+    lax.fori_loop(0, DEEP + 1, make_spread, 0)
     wide = lax.broadcasted_iota(jnp.int32, (COLS, TILES * LANES), 1)
     tall = lax.broadcasted_iota(jnp.int32, (COLS, TILES * LANES), 0)
     perm_m[...] = one_hot((tall + HALO == lax.rem(wide, SIDE) * DEEP + wide // SIDE) & (wide < SIDE * DEEP))
@@ -308,18 +318,20 @@
         return values
 
     def spread_angles(blocks):
-        def spread_orb(orb, carry):
+        def spread_orbs(pair, carry):
+            orbs = [2 * pair, 2 * pair + 1]
+            places = [(orb, block) for orb in orbs for block in blocks]
             value = jnp.concatenate(
                 [
                     jnp.concatenate(
                         [ang[t, :, orb, pl.ds(8 * block, 8), :].reshape(STATES * 8, LANES) for t in range(2)], axis=1
                     )
-                    for block in blocks
+                    for orb, block in places
                 ],
                 axis=0,
             )
             out = moved(value, perm_m[...])
-            for which, block in enumerate(blocks):
+            for which, (orb, block) in enumerate(places):
                 parts = [
                     [
                         out[64 * which + 8 * r : 64 * which + 8 * r + 8, LANES * t : LANES * t + LANES]
@@ -335,7 +347,7 @@
                     af[orb, y, pl.ds(8 * block, 8), :] = value
             return carry
 
-        lax.fori_loop(0, 4, spread_orb, 0)
+        lax.fori_loop(0, 2, spread_orbs, 0)
 
     spread_angles((1, 2))
 
@@ -404,32 +416,35 @@
         i = sub_i + 8 * block
         return (j >= 0) & (j < ny) & (i >= 0) & (i < nx)
 
-    def make_tables(y, carry):
-        out = jnp.dot(
+    def make_tables(pair, carry):
+        two = jnp.dot(
             planes,
-            spread_m[:, pl.ds(pl.multiple_of(y * LANES, LANES), LANES)],
+            spread_m[:, pl.ds(pl.multiple_of(pair * (2 * LANES), 2 * LANES), 2 * LANES)],
             preferred_element_type=jnp.float32,
         )
-        place = lane_place + y
-        j = gy * COLS - HALO + place
-        for block in range(BLOCKS):
-            rows = pl.ds(ROW0 + 8 * block, 8)
-            part = [out[which * EXT + 8 * block : which * EXT + 8 * block + 8, :] for which in range(10)]
-            for orb in range(4):
-                phf[orb, y, pl.ds(8 * block, 8), :] = part[orb] * (1.0 / QUANTA)
-            here = cell_inside(y, block)
-            for which, good in (
-                (T2C, here & (j >= 1) & (place >= 1)),
-                (T4C, here & (sub_i + 8 * block + 1 < nx)),
-                (T5C, here & (j + 1 < ny) & (place < SIDE * DEEP - 1)),
-            ):
-                c, s = turn(part[4 + which // 2] * (1.0 / QUANTA))
-                ft[which, y + 1, rows, :] = jnp.where(good, c, 0.0)
-                ft[which + 1, y + 1, rows, :] = jnp.where(good, s, 0.0)
-            ft[CPL, y + 1, rows, :] = jnp.where(here, part[7] + part[8] + part[9], 0.0)
+        for one in range(2):
+            y = 2 * pair + one
+            out = two[:, LANES * one : LANES * one + LANES]
+            place = lane_place + y
+            j = gy * COLS - HALO + place
+            for block in range(BLOCKS):
+                rows = pl.ds(ROW0 + 8 * block, 8)
+                part = [out[which * EXT + 8 * block : which * EXT + 8 * block + 8, :] for which in range(10)]
+                for orb in range(4):
+                    phf[orb, y, pl.ds(8 * block, 8), :] = part[orb] * (1.0 / QUANTA)
+                here = cell_inside(y, block)
+                for which, good in (
+                    (T2C, here & (j >= 1) & (place >= 1)),
+                    (T4C, here & (sub_i + 8 * block + 1 < nx)),
+                    (T5C, here & (j + 1 < ny) & (place < SIDE * DEEP - 1)),
+                ):
+                    c, s = small_turn(part[4 + which // 2], QUANTA)
+                    ft[which, y + 1, rows, :] = jnp.where(good, c, 0.0)
+                    ft[which + 1, y + 1, rows, :] = jnp.where(good, s, 0.0)
+                ft[CPL, y + 1, rows, :] = jnp.where(here, part[7] + part[8] + part[9], 0.0)
         return carry
 
-    lax.fori_loop(0, DEEP, make_tables, 0)
+    lax.fori_loop(0, (DEEP + 1) // 2, make_tables, 0)
     for block in range(BLOCKS):
         rows = pl.ds(ROW0 + 8 * block, 8)
         for which in (T2C, T2S):
@@ -438,22 +453,24 @@
             ft[which, 0, rows, :] = pltpu.roll(ft[which, DEEP, rows, :], 1, 1)
 
     def start_values(blocks):
-        def start_one(y, carry):
-            place = lane_place + y
-            beyond = (place < HALO) | (place >= COLS + HALO)
-            move = jnp.where(y <= HALO, LANES - HALO - y, SIDE + HALO - y)
-            for block in blocks:
-                here = cell_inside(y, block)
-                rows = pl.ds(8 * block, 8)
-                for orb in range(4):
-                    angle = jnp.where(beyond, pltpu.roll(unpack(orb, block), move, 1), af[orb, y, rows, :])
-                    c, s = turn(angle * (0.5 / math.pi) + phf[orb, y, rows, :])
-                    size = 2.0 if orb in (A1, A2) else 1.0
-                    u[0, 2 * orb, y + 1, pl.ds(ROW0 + 8 * block, 8), :] = jnp.where(here, size * c, 0.0)
-                    u[0, 2 * orb + 1, y + 1, pl.ds(ROW0 + 8 * block, 8), :] = jnp.where(here, size * s, 0.0)
+        def start_one(pair, carry):
+            for y in (2 * pair, 2 * pair + 1):
+                place = lane_place + y
+                beyond = (place < HALO) | (place >= COLS + HALO)
+                move = jnp.where(y <= HALO, LANES - HALO - y, SIDE + HALO - y)
+                for block in blocks:
+                    here = cell_inside(y, block)
+                    rows = pl.ds(8 * block, 8)
+                    for orb in range(4):
+                        angle = jnp.where(beyond, pltpu.roll(unpack(orb, block), move, 1), af[orb, y, rows, :])
+                        c, s = turn(
+                            angle * (0.5 / math.pi) + phf[orb, y, rows, :], 2.0 if orb in (A1, A2) else 1.0
+                        )
+                        u[0, 2 * orb, y + 1, pl.ds(ROW0 + 8 * block, 8), :] = jnp.where(here, c, 0.0)
+                        u[0, 2 * orb + 1, y + 1, pl.ds(ROW0 + 8 * block, 8), :] = jnp.where(here, s, 0.0)
             return carry
 
-        lax.fori_loop(0, DEEP, start_one, 0)
+        lax.fori_loop(0, (DEEP + 1) // 2, start_one, 0)
 
     start_values((1, 2))
     for what, copy in row_copies:
@@ -532,12 +549,15 @@
                 u[dst, 2 * orb + part, y + 1, rows, :] = value
 
     def step(src, dst, rows, first=False):
-        def step_one(y, carry):
+        def step_two(pair, carry):
             for row in rows:
-                step_at(src, dst, y, row, first)
+                step_at(src, dst, 2 * pair, row, first)
+                step_at(src, dst, 2 * pair + 1, row, first)
             return carry
 
-        lax.fori_loop(0, DEEP, step_one, 0, unroll=UNROLL)
+        for row in rows:
+            step_at(src, dst, DEEP - 1, row, first)
+        lax.fori_loop(0, DEEP // 2, step_two, 0)
         for row in rows:
             join(dst, row)
 
@@ -554,7 +574,7 @@
                     u[dst, 2 * orb + part, :, pl.ds(ROW0 + HALO + ROWS, 1), :] = jnp.zeros((DEEP + 2, 1, LANES), jnp.float32)
 
     def gather(k):
-        def gather_one(y, sums):
+        def gather_at(y, sums):
             sums = list(sums)
             for block in range(2):
                 for orb in range(4):
@@ -566,7 +586,10 @@
                         sums[2 * which + 1] += vr * ui - vi * ur
             return tuple(sums)
 
-        sums = lax.fori_loop(0, DEEP, gather_one, (zero,) * 4)
+        def gather_two(pair, sums):
+            return gather_at(2 * pair + 1, gather_at(2 * pair, sums))
+
+        sums = gather_at(DEEP - 1, lax.fori_loop(0, DEEP // 2, gather_two, (zero,) * 4))
         for which in range(4):
             mom[2 * k + which] = sums[which]
 
@@ -722,10 +745,10 @@
             pltpu.VMEM((2, 8, DEEP + 2, EXT + 2 * ROW0, LANES), f32),
             pltpu.VMEM((TERMS, DEEP, 2, 8) + tile, f32),
             pltpu.VMEM((7, DEEP + 2, EXT + 2 * ROW0, LANES), f32),
-            pltpu.VMEM((4, DEEP, EXT, LANES), f32),
-            pltpu.VMEM((4, DEEP, EXT, LANES), f32),
+            pltpu.VMEM((4, DEEP + 1, EXT, LANES), f32),
+            pltpu.VMEM((4, DEEP + 1, EXT, LANES), f32),
             pltpu.VMEM((10, EXT, TILES * LANES), f32),
-            pltpu.VMEM((TILES * LANES, DEEP * LANES), jnp.bfloat16),
+            pltpu.VMEM((TILES * LANES, (DEEP + 1) * LANES), jnp.bfloat16),
             pltpu.VMEM((COLS, TILES * LANES), jnp.bfloat16),
             pltpu.VMEM((TILES * LANES, COLS), jnp.bfloat16),
             pltpu.VMEM((4, 2, 2, ROWS, LANES), f32),

time: 60.7 us -> 55.1 us (0.908)
  Pallas kernels: 57 us -> 51.4 us
    pallas_call x1, Pallas kernels: 57 us -> 51.4 us  [per_device(): pl.pallas_call(functools.partial(kernel, nx, ny, gx_size, gy_size), out_s...]
where the time goes in v3:
time: 55.1 us; the launch traced here: 55 us
  Pallas kernels  51.4 us (93%)
  local copies, waits for them, and re-layouts  2.9 us (5%)
  between operations  0.65 us (1%)
    pallas_call x1, Pallas kernels, per_device(): pl.pallas_call(functools.partial(kernel, nx, ny, gx_size, gy_size), out_s...  51.4 us
    unnamed x4, local copies, waits for them, and re-layouts  2.9 us

profile of v3, /device:TPU:1, one launch (start us, length us, event | category | flops | bytes accessed | tf_op | source)
XLA Modules:
  0.0 55.0 jit_solution(17369794498690666976)
XLA Ops:
  0.6 51.4 %evolve.1 = (f32[2,8,4,16,256]{4,3,2,1,0:T(8,128)}, f32[2,8,16]{2,1,0:T(8,128)}) custom-call(f32[8,4,16,256]{3,2,1,0:T(8,128)} %ang_h.1, s32[7,16,256]{2,1,0:T(8,128)} %flux_h.1, f32[16,256]{1,0:T(8,128)} %coup_h.1), custom_call_target="tpu_custom_call" | custom-call | tf_op jit(solution)/shard_map/evolve/pallas_call | solution.py:733
  52.1 0.0 copy-start
  52.1 2.3 %copy.7 = f32[2,8,4,16,256]{4,3,2,1,0:T(8,128)} copy(f32[2,8,4,16,256]{4,3,2,1,0:T(8,128)} %get-tuple-element.8) | data formatting | bytes 2097152
  54.4 0.0 copy-done
  54.4 0.6 %copy.8 = f32[16,2,8]{0,2,1:T(8,128)} copy(f32[16,2,8]{0,2,1:T(8,128)S(1)} %bitcast.1) | data formatting | bytes 2048
Async XLA Ops:
  52.1 2.3 %copy-start = (f32[2,8,16]{2,1,0:T(8,128)S(1)}, f32[2,8,16]{2,1,0:T(8,128)}, u32[]{:S(2)}) copy-start(f32[2,8,16]{2,1,0:T(8,128)} %get-tuple-element.5) | copy-start | bytes 3076

commit v4 on v3

--- a/solution.py
+++ b/solution.py
@@ -90,7 +90,7 @@
 def kernel(
     nx, ny, gx_size, gy_size,
     ang_h, flux_h, coup_h, evo_h, mom_ref,
-    ang, fli, flf, u, hist, ft, phf, af, px, spread_m, perm_m, back_m, gauge, chi, vel, tf, tl, outv, mom, pack, got, msg_1, msg_2, in_1, in_2,
+    ang, fli, flf, u, hist, ft, phf, af, px, spread_m, perm_m, back_m, gauge, chi, vel, tf, tl, outv, mom, pack, msg_own, msg_far, got_own, got_far, halo, msg_1, msg_2, in_1, in_2,
     load_sem, out_sem, xs_sem, xr_sem, ps_sem, pr_sem, s1_sem, r1_sem, s2_sem, r2_sem,
 ):
     gx, gy = lax.axis_index("gx"), lax.axis_index("gy")
@@ -176,59 +176,16 @@
         for block in range(2):
             pack[side, block, 4] = packed(side, lambda r: flf[1 - side, pl.ds(r * PAD + HALO + 8 * block, 8), :])
 
-    pl.semaphore_wait(barrier, 8 + group_1 - 1 + group_2 - 1)
-
-    row_copies = []
-    for side, dx in ((0, 1), (1, -1)):
-        src_rows = pl.ds(ROWS - HALO, HALO) if side == 0 else pl.ds(0, HALO)
-        low = 0 if side == 0 else HALO + ROWS
-        for t in range(2):
-            span = pl.ds(t * LANES, LANES)
-            for what, (src, dst) in enumerate(
-                (
-                    (flux_h.at[:, src_rows, span], fli.at[t, :, pl.ds(low, HALO), :]),
-                    (coup_h.at[src_rows, span], flf.at[t, pl.ds(7 * PAD + low, HALO), :]),
-                    (ang_h.at[:, :, src_rows, span], ang.at[t, :, :, pl.ds(low, HALO), :]),
-                )
-            ):
-                row_copies.append(
-                    (
-                        what,
-                        pltpu.make_async_remote_copy(
-                            src_ref=src,
-                            dst_ref=dst,
-                            send_sem=xs_sem.at[side, t, what],
-                            recv_sem=xr_sem.at[side, t, what],
-                            device_id=near(dx, 0),
-                            device_id_type=MESH,
-                        ),
-                    )
-                )
-    pack_copies = []
-    for side, dy in ((0, 1), (1, -1)):
-        for dx, src, dst in (
-            (0, pack.at[side], got.at[side, pl.ds(1, 2)]),
-            (1, pack.at[side, 1], got.at[side, 0]),
-            (-1, pack.at[side, 0], got.at[side, 3]),
-        ):
-            pack_copies.append(
-                pltpu.make_async_remote_copy(
-                    src_ref=src,
-                    dst_ref=dst,
-                    send_sem=ps_sem.at[side, 1 - dx],
-                    recv_sem=pr_sem.at[side, 1 - dx],
-                    device_id=near(dx, dy),
-                    device_id_type=MESH,
-                )
-            )
-    for what, copy in row_copies:
-        if what < 2:
-            copy.start()
-    for copy in pack_copies:
-        copy.start()
-    for what, copy in row_copies:
-        if what == 2:
-            copy.start()
+    def pushed(value, side):
+        return pltpu.roll(value, LANES - HALO if side == 0 else HALO, 1)
+
+    for side in range(2):
+        for what in range(5):
+            msg_own[side, what] = pack[side, 0, what] + pushed(pack[side, 1, what], side)
+        for block in range(2):
+            for what in range(2):
+                msg_far[side, block, what] = pack[side, block, 2 * what] + pushed(pack[side, block, 2 * what + 1], side)
+            msg_far[side, block, 2] = pack[side, block, 4]
 
     def flux_of(t, plane, start, count=8):
         return flf[t, pl.ds(plane * PAD + start, count), :]
@@ -351,6 +308,69 @@
 
     spread_angles((1, 2))
 
+    pl.semaphore_wait(barrier, 8 + group_1 - 1 + group_2 - 1)
+
+    row_copies = []
+    for side, dx in ((0, 1), (1, -1)):
+        src_rows = pl.ds(ROWS - HALO, HALO) if side == 0 else pl.ds(0, HALO)
+        low = 0 if side == 0 else HALO + ROWS
+        for t in range(2):
+            span = pl.ds(t * LANES, LANES)
+            for what, (src, dst) in enumerate(
+                (
+                    (flux_h.at[:, src_rows, span], fli.at[t, :, pl.ds(low, HALO), :]),
+                    (coup_h.at[src_rows, span], flf.at[t, pl.ds(7 * PAD + low, HALO), :]),
+                    (ang_h.at[:, :, src_rows, span], ang.at[t, :, :, pl.ds(low, HALO), :]),
+                )
+            ):
+                row_copies.append(
+                    (
+                        what,
+                        pltpu.make_async_remote_copy(
+                            src_ref=src,
+                            dst_ref=dst,
+                            send_sem=xs_sem.at[side, t, what],
+                            recv_sem=xr_sem.at[side, t, what],
+                            device_id=near(dx, 0),
+                            device_id_type=MESH,
+                        ),
+                    )
+                )
+    pack_copies = []
+    for side, dy in ((0, 1), (1, -1)):
+        for dx, src, dst, cut in (
+            (0, msg_own.at[side], got_own.at[side], 4),
+            (1, msg_far.at[side, 1], got_far.at[side, 0], 2),
+            (-1, msg_far.at[side, 0], got_far.at[side, 1], 2),
+        ):
+            for late, part in enumerate((pl.ds(cut, 1), pl.ds(0, cut))):
+                pack_copies.append(
+                    (
+                        late,
+                        pltpu.make_async_remote_copy(
+                            src_ref=src.at[part],
+                            dst_ref=dst.at[part],
+                            send_sem=ps_sem.at[side, 1 - dx, late],
+                            recv_sem=pr_sem.at[side, 1 - dx, late],
+                            device_id=near(dx, dy),
+                            device_id_type=MESH,
+                        ),
+                    )
+                )
+    for late, copy in pack_copies:
+        if not late:
+            copy.start()
+    for what, copy in row_copies:
+        if what < 2:
+            copy.start()
+    for late, copy in pack_copies:
+        if late:
+            copy.start()
+    for what, copy in row_copies:
+        if what == 2:
+            copy.start()
+
+
     for what, copy in row_copies:
         if what < 2:
             copy.wait()
@@ -358,16 +378,28 @@
         for start in (0, HALO + ROWS):
             flux_to_float(t, start, HALO)
             cell_phases(t, start, carries[t])
-    for copy in pack_copies:
-        copy.wait()
+    for late, copy in pack_copies:
+        if not late:
+            copy.wait()
 
     beside = lax.rem(lane, SIDE)
 
-    def unpack(what, block):
-        return jnp.where(beside < HALO, got[1, block, what], got[0, block, what])
+    def pulled(value, side):
+        return pltpu.roll(value, HALO if side == 0 else LANES - HALO, 1)
+
+    def merge(what, block):
+        sides = []
+        for side in range(2):
+            if block in (1, 2):
+                value = got_own[side, what]
+                sides.append(pulled(value, side) if block == 2 else value)
+            else:
+                value = got_far[side, 0 if block == 0 else 1, 2 if what == 4 else what // 2]
+                sides.append(pulled(value, side) if what in (1, 3) else value)
+        return jnp.where(beside < HALO, sides[1], sides[0])
 
     for block in range(BLOCKS):
-        values = unpack(4, block)
+        values = merge(4, block)
         for which in range(8):
             move = (LANES - SIDE * which) % LANES
             flf[2, pl.ds(which * PAD + 8 * block, 8), :] = pltpu.roll(values, move, 1) if move else values
@@ -462,7 +494,7 @@
                     here = cell_inside(y, block)
                     rows = pl.ds(8 * block, 8)
                     for orb in range(4):
-                        angle = jnp.where(beyond, pltpu.roll(unpack(orb, block), move, 1), af[orb, y, rows, :])
+                        angle = jnp.where(beyond, pltpu.roll(halo[block, orb], move, 1), af[orb, y, rows, :])
                         c, s = turn(
                             angle * (0.5 / math.pi) + phf[orb, y, rows, :], 2.0 if orb in (A1, A2) else 1.0
                         )
@@ -472,6 +504,12 @@
 
         lax.fori_loop(0, (DEEP + 1) // 2, start_one, 0)
 
+    for late, copy in pack_copies:
+        if late:
+            copy.wait()
+    for block in range(BLOCKS):
+        for orb in range(4):
+            halo[block, orb] = merge(orb, block)
     start_values((1, 2))
     for what, copy in row_copies:
         if what == 2:
@@ -675,7 +713,7 @@
         return pltpu.make_async_copy(outv.at[:, :, orb], evo_h.at[:, :, orb], out_sem.at[orb])
 
     def evolve(orb, carry):
-        def evolve_one(y, carry):
+        def evolve_at(y):
             for block in range(2):
                 re, im = zero, zero
                 for m in range(TERMS // 2):
@@ -683,9 +721,14 @@
                     re = re + (EVEN[m] * a[0] - ODD[m] * b[1])
                     im = im + (EVEN[m] * a[1] + ODD[m] * b[0])
                 tf[block, y], tf[2 + block, y] = re, im
+
+        def evolve_two(pair, carry):
+            evolve_at(2 * pair)
+            evolve_at(2 * pair + 1)
             return carry
 
-        lax.fori_loop(0, DEEP, evolve_one, 0)
+        evolve_at(DEEP - 1)
+        lax.fori_loop(0, DEEP // 2, evolve_two, 0)
 
         def back(which, carry):
             tiles = [exchanged([tf[which, 8 * t + i] for i in range(8)]) for t in range(2)]
@@ -759,7 +802,11 @@
             pltpu.VMEM((2, STATES, 4, ROWS, COLS), f32),
             pltpu.VMEM((2 * TERMS,) + tile, f32),
             pltpu.VMEM((2, 2, 5) + tile, f32),
-            pltpu.VMEM((2, BLOCKS, 5) + tile, f32),
+            pltpu.VMEM((2, 5) + tile, f32),
+            pltpu.VMEM((2, 2, 3) + tile, f32),
+            pltpu.VMEM((2, 5) + tile, f32),
+            pltpu.VMEM((2, 2, 3) + tile, f32),
+            pltpu.VMEM((BLOCKS, 4) + tile, f32),
             pltpu.VMEM((2, LANES), f32),
             pltpu.VMEM((2, LANES), f32),
             pltpu.VMEM((group_1, 2, LANES), f32),
@@ -768,8 +815,8 @@
             pltpu.SemaphoreType.DMA((4,)),
             pltpu.SemaphoreType.DMA((2, 2, 3)),
             pltpu.SemaphoreType.DMA((2, 2, 3)),
-            pltpu.SemaphoreType.DMA((2, 3)),
-            pltpu.SemaphoreType.DMA((2, 3)),
+            pltpu.SemaphoreType.DMA((2, 3, 2)),
+            pltpu.SemaphoreType.DMA((2, 3, 2)),
             pltpu.SemaphoreType.DMA((group_1,)),
             pltpu.SemaphoreType.DMA((group_1,)),
             pltpu.SemaphoreType.DMA((group_2,)),

time: 55.1 us -> 52.5 us (0.953)
  Pallas kernels: 51.4 us -> 48.8 us
    pallas_call x1, Pallas kernels: 51.4 us -> 48.8 us  [per_device(): pl.pallas_call(functools.partial(kernel, nx, ny, gx_size, gy_size), out_s...]
where the time goes in v4:
time: 52.5 us; the launch traced here: 52.4 us
  Pallas kernels  48.8 us (93%)
  local copies, waits for them, and re-layouts  2.9 us (6%)
  between operations  0.65 us (1%)
    pallas_call x1, Pallas kernels, per_device(): pl.pallas_call(functools.partial(kernel, nx, ny, gx_size, gy_size), out_s...  48.8 us
    unnamed x4, local copies, waits for them, and re-layouts  2.9 us

profile of v4, /device:TPU:1, one launch (start us, length us, event | category | flops | bytes accessed | tf_op | source)
XLA Modules:
  0.0 52.4 jit_solution(2549860459903085876)
XLA Ops:
  0.6 48.8 %evolve.1 = (f32[2,8,4,16,256]{4,3,2,1,0:T(8,128)}, f32[2,8,16]{2,1,0:T(8,128)}) custom-call(f32[8,4,16,256]{3,2,1,0:T(8,128)} %ang_h.1, s32[7,16,256]{2,1,0:T(8,128)} %flux_h.1, f32[16,256]{1,0:T(8,128)} %coup_h.1), custom_call_target="tpu_custom_call" | custom-call | tf_op jit(solution)/shard_map/evolve/pallas_call | solution.py:776
  49.5 0.0 copy-start
  49.5 2.3 %copy.7 = f32[2,8,4,16,256]{4,3,2,1,0:T(8,128)} copy(f32[2,8,4,16,256]{4,3,2,1,0:T(8,128)} %get-tuple-element.8) | data formatting | bytes 2097152
  51.8 0.0 copy-done
  51.8 0.6 %copy.8 = f32[16,2,8]{0,2,1:T(8,128)} copy(f32[16,2,8]{0,2,1:T(8,128)S(1)} %bitcast.1) | data formatting | bytes 2048
Async XLA Ops:
  49.5 2.3 %copy-start = (f32[2,8,16]{2,1,0:T(8,128)S(1)}, f32[2,8,16]{2,1,0:T(8,128)}, u32[]{:S(2)}) copy-start(f32[2,8,16]{2,1,0:T(8,128)} %get-tuple-element.5) | copy-start | bytes 3076

commit v5 on v4

--- a/solution.py
+++ b/solution.py
@@ -586,7 +586,7 @@
                     value = (value if size == 1.0 else size * value) - u[dst, 2 * orb + part, y + 1, rows, :]
                 u[dst, 2 * orb + part, y + 1, rows, :] = value
 
-    def step(src, dst, rows, first=False):
+    def step(src, dst, rows, first=False, last=False):
         def step_two(pair, carry):
             for row in rows:
                 step_at(src, dst, 2 * pair, row, first)
@@ -596,6 +596,8 @@
         for row in rows:
             step_at(src, dst, DEEP - 1, row, first)
         lax.fori_loop(0, DEEP // 2, step_two, 0)
+        if last:
+            return
         for row in rows:
             join(dst, row)
 
@@ -642,15 +644,15 @@
         return carry
 
     def late(m, carry):
-        step(1, 0, mid_rows)
         step(0, 1, mid_rows)
         gather(2 * m)
+        step(1, 0, mid_rows)
         return carry
 
-    lax.fori_loop(1, 4, early, 0)
-    lax.fori_loop(4, TERMS // 2 - 1, late, 0)
-    step(1, 0, mid_rows)
-    step(0, 1, own_rows)
+    lax.fori_loop(1, 3, early, 0)
+    step(1, 0, far_rows)
+    lax.fori_loop(3, TERMS // 2 - 1, late, 0)
+    step(0, 1, own_rows, last=True)
     gather(TERMS - 2)
 
     sums = []

time: 52.5 us -> 52.2 us (level)
  no operation moved by 1% of the time
where the time goes in v5:
time: 52.2 us; the launch traced here: 52.1 us
  Pallas kernels  48.6 us (93%)
  local copies, waits for them, and re-layouts  2.9 us (6%)
  between operations  0.65 us (1%)
    pallas_call x1, Pallas kernels, per_device(): pl.pallas_call(functools.partial(kernel, nx, ny, gx_size, gy_size), out_s...  48.6 us
    unnamed x4, local copies, waits for them, and re-layouts  2.9 us

profile of v5, /device:TPU:1, one launch (start us, length us, event | category | flops | bytes accessed | tf_op | source)
XLA Modules:
  0.0 52.1 jit_solution(11983301225711858710)
XLA Ops:
  0.6 48.6 %evolve.1 = (f32[2,8,4,16,256]{4,3,2,1,0:T(8,128)}, f32[2,8,16]{2,1,0:T(8,128)}) custom-call(f32[8,4,16,256]{3,2,1,0:T(8,128)} %ang_h.1, s32[7,16,256]{2,1,0:T(8,128)} %flux_h.1, f32[16,256]{1,0:T(8,128)} %coup_h.1), custom_call_target="tpu_custom_call" | custom-call | tf_op jit(solution)/shard_map/evolve/pallas_call | solution.py:778
  49.2 0.0 copy-start
  49.2 2.3 %copy.7 = f32[2,8,4,16,256]{4,3,2,1,0:T(8,128)} copy(f32[2,8,4,16,256]{4,3,2,1,0:T(8,128)} %get-tuple-element.8) | data formatting | bytes 2097152
  51.5 0.0 copy-done
  51.5 0.6 %copy.8 = f32[16,2,8]{0,2,1:T(8,128)} copy(f32[16,2,8]{0,2,1:T(8,128)S(1)} %bitcast.1) | data formatting | bytes 2048
Async XLA Ops:
  49.2 2.3 %copy-start = (f32[2,8,16]{2,1,0:T(8,128)S(1)}, f32[2,8,16]{2,1,0:T(8,128)}, u32[]{:S(2)}) copy-start(f32[2,8,16]{2,1,0:T(8,128)} %get-tuple-element.5) | copy-start | bytes 3076
